TPU v7x, 32 devices: a whole 2x2x4 slice. The times are simulated.
32 devices in a mesh: slide: 4 (over z), ctx: 8 (over y, x, core).
Axes of the slice: x: 2, y: 2, z: 4, core: 2. Of those that a mesh axis runs over, the one named last changes fastest.
Arguments:
- tiles: bfloat16 [4, 4096, 768], P('slide', 'ctx'), may hold values from -40 to 40
- tile_pos: int32 [4, 4096], P('slide', 'ctx'), may hold values from 0 to 4095, as said below
- lengths: int32 [4], P('slide'), may hold values from 1024 to 4096, as said below
- qkv_weight: bfloat16 [768, 1152], replicated, may hold values from -0.21875 to 0.21875
- out_weight: bfloat16 [384, 768], replicated, may hold values from -0.3125 to 0.3125
- cotangent: bfloat16 [4, 4096, 768], P('slide', 'ctx'), may hold values from -6 to 6
Outputs:
- tile_grads: bfloat16 [4, 4096, 768], P('slide', 'ctx')
- out_weight_grad: float32 [294912], P(('slide', 'ctx'))
- far_kv_grads: float32 [4, 2, 6, 256, 64], P('slide', None, None, 'ctx')
Inputs may be any that keep to these rules, and one draw needn't show every extreme that they name: `tile_pos`: for every slide the entries are a permutation of its 4096 positions; the 512 entries held by one device of ctx contain exactly 64 positions of each block of 512 consecutive positions, in no particular order. `lengths`: at least one slide has all 4096 positions live.
All inputs are finite; a program needn't handle non-finite values.
Results may differ from a plain program's by a relative error of at most 0.014.
The roundings to bfloat16 on the way count: a program that leaves them out, or rounds other values in their place, can miss the bound.
Values may be sent and summed in bfloat16 or wider, within the bound.
A program may use at most 128 MiB of HBM per device.

v0:
```python
import math

import jax
import jax.numpy as jnp
from jax import lax
from jax.sharding import PartitionSpec as P

HD = 64
WIDE_RATE2 = 16


NEGATIVE_FLOOR = -1e30


def dilate(tensor, stride):
    number = tensor.shape[1]
    lattice = tensor.reshape(tensor.shape[0] // stride, stride, number, tensor.shape[2])
    return jnp.stack([lattice[:, offset, offset, :] for offset in range(number)], 0)


def selector(number, stride):
    return jnp.arange(stride)[None, :] == jnp.arange(number)[:, None]


def spread(values, stride, filler):
    chosen = selector(values.shape[0], stride)
    return jnp.where(chosen[:, None, :], values[:, :, None], filler).reshape(values.shape[0], -1)


def spread_rows(values, stride):
    chosen = selector(values.shape[0], stride)
    placed = jnp.where(chosen[:, None, :, None], values[:, :, None, :], 0.0)
    return placed.reshape(values.shape[0], -1, values.shape[2])


def extract(field, stride):
    chosen = selector(field.shape[0], stride)
    lattice = field.reshape(field.shape[0], -1, stride)
    return jnp.sum(jnp.where(chosen[:, None, :], lattice, 0.0), -1)


def extract_rows(field, stride):
    chosen = selector(field.shape[0], stride)
    lattice = field.reshape(field.shape[0], -1, stride, field.shape[2])
    return jnp.sum(jnp.where(chosen[:, None, :, None], lattice, 0.0), 2)


def local(tiles, tile_pos, lengths, qkv_weight, out_weight, cotangent):
    row_count = tiles.shape[1]
    features = tiles.shape[2]
    peer_count = lax.axis_size("ctx")
    device = lax.axis_index("ctx")
    portion = row_count // peer_count
    number = out_weight.shape[0] // HD
    stride = WIDE_RATE2
    groups = row_count // stride
    places = tile_pos[0]
    ordering = jnp.argsort(places // row_count, stable=True)
    sent_rows = tiles[0][ordering].reshape(peer_count, portion, features)
    sent_places = places[ordering].reshape(peer_count, portion)
    got_rows, got_places = (
        lax.all_to_all(sent_rows, "ctx", split_axis=0, concat_axis=0, tiled=True),
        lax.all_to_all(sent_places, "ctx", split_axis=0, concat_axis=0, tiled=True),
    )
    slot_index = got_places.reshape(row_count) - device * row_count
    sequence = (
        jnp.zeros((row_count, features), jnp.bfloat16)
        .at[slot_index]
        .set(got_rows.reshape(row_count, features))
    )
    projected = jnp.dot(sequence, qkv_weight, preferred_element_type=jnp.float32).astype(
        jnp.bfloat16
    )
    projected = projected.reshape(row_count, 3, number, HD)
    queries = projected[:, 0]
    keyset = projected[:, 1]
    values = projected[:, 2]
    slide_length = lengths[0]
    live_rows = device * row_count + jnp.arange(row_count) < slide_length
    local_scores = (
        jnp.einsum("qhd,khd->hqk", queries, keyset, preferred_element_type=jnp.float32) * 0.125
    )
    local_masked = jnp.where(live_rows[None, None, :], local_scores, NEGATIVE_FLOOR)
    local_max = jnp.max(local_masked, -1)
    near_query = dilate(queries, stride)
    near_keys = dilate(keyset, stride)
    near_values = dilate(values, stride)
    far_keys, far_values = (
        lax.all_gather(near_keys, "ctx", axis=1, tiled=True),
        lax.all_gather(near_values, "ctx", axis=1, tiled=True),
    )
    head_offsets = jnp.arange(number)[:, None]
    far_live = jnp.arange(groups * peer_count)[None, :] * stride + head_offsets < slide_length
    distant_scores = (
        jnp.einsum("hqd,hkd->hqk", near_query, far_keys, preferred_element_type=jnp.float32) * 0.125
    )
    distant_masked = jnp.where(far_live[:, None, :], distant_scores, NEGATIVE_FLOOR)
    far_max = jnp.max(distant_masked, -1)
    ceiling = jnp.maximum(local_max, spread(far_max, stride, NEGATIVE_FLOOR))
    local_weights = jnp.where(
        live_rows[None, None, :], jnp.exp(local_masked - ceiling[:, :, None]), 0.0
    )
    distant_ceiling = extract(ceiling, stride)
    distant_weights = jnp.where(
        far_live[:, None, :], jnp.exp(distant_masked - distant_ceiling[:, :, None]), 0.0
    )
    totals = jnp.sum(local_weights, -1) + spread(jnp.sum(distant_weights, -1), stride, 0.0)
    local_numer = jnp.einsum(
        "hqk,khd->hqd",
        local_weights.astype(jnp.bfloat16),
        values,
        preferred_element_type=jnp.float32,
    )
    far_numer = jnp.einsum(
        "hqk,hkd->hqd",
        distant_weights.astype(jnp.bfloat16),
        far_values,
        preferred_element_type=jnp.float32,
    )
    numerator = local_numer + spread_rows(far_numer, stride)
    divisor = jnp.where(live_rows[None, :], totals, 1.0)
    result = jnp.where(live_rows[None, :, None], numerator / divisor[:, :, None], 0.0)
    attention = result.transpose(1, 0, 2).reshape(row_count, number * HD).astype(jnp.bfloat16)
    grad_seq = cotangent[0]
    factor = 1.0 / math.sqrt(lax.axis_size("slide") * peer_count * row_count)
    partial_term = (
        jnp.einsum("qc,qd->cd", attention, grad_seq, preferred_element_type=jnp.float32) * factor
    )
    weight_grad = lax.psum_scatter(
        partial_term.reshape(-1), ("slide", "ctx"), scatter_dimension=0, tiled=True
    )
    grad_attn = jnp.einsum(
        "qd,cd->qc", grad_seq, out_weight, preferred_element_type=jnp.float32
    ).astype(jnp.bfloat16)
    grad_attn = grad_attn.reshape(row_count, number, HD)
    grad_out = jnp.where(
        live_rows[:, None, None], grad_attn, jnp.zeros((), jnp.bfloat16)
    ).transpose(1, 0, 2)
    inner_stat = jnp.sum(grad_out.astype(jnp.float32) * result, -1)
    local_prob = local_weights / divisor[:, :, None]
    local_dprob = jnp.einsum("hqd,khd->hqk", grad_out, values, preferred_element_type=jnp.float32)
    local_dscore = (local_prob * (local_dprob - inner_stat[:, :, None]) * 0.125).astype(
        jnp.bfloat16
    )
    grad_query = jnp.einsum(
        "hqk,khd->hqd", local_dscore, keyset, preferred_element_type=jnp.float32
    )
    grad_key = jnp.einsum("hqk,qhd->hkd", local_dscore, queries, preferred_element_type=jnp.float32)
    grad_value = jnp.einsum(
        "hqk,hqd->hkd",
        local_prob.astype(jnp.bfloat16),
        grad_out,
        preferred_element_type=jnp.float32,
    )
    near_divisor = extract(divisor, stride)
    near_stat = extract(inner_stat, stride)
    near_grad = extract_rows(grad_out.astype(jnp.float32), stride).astype(jnp.bfloat16)
    far_prob = distant_weights / near_divisor[:, :, None]
    far_dprob = jnp.einsum(
        "hqd,hkd->hqk", near_grad, far_values, preferred_element_type=jnp.float32
    )
    far_dscore = (far_prob * (far_dprob - near_stat[:, :, None]) * 0.125).astype(jnp.bfloat16)
    far_qgrad = jnp.einsum("hqk,hkd->hqd", far_dscore, far_keys, preferred_element_type=jnp.float32)
    grad_query = grad_query + spread_rows(far_qgrad, stride)
    partial_keys = jnp.einsum(
        "hqk,hqd->hkd", far_dscore, near_query, preferred_element_type=jnp.float32
    )
    partial_values = jnp.einsum(
        "hqk,hqd->hkd", far_prob.astype(jnp.bfloat16), near_grad, preferred_element_type=jnp.float32
    )
    owned_kgrad, owned_vgrad = (
        lax.psum_scatter(partial_keys, "ctx", scatter_dimension=1, tiled=True),
        lax.psum_scatter(partial_values, "ctx", scatter_dimension=1, tiled=True),
    )
    grad_key = grad_key + spread_rows(owned_kgrad, stride)
    grad_value = grad_value + spread_rows(owned_vgrad, stride)
    far_pair = jnp.stack([owned_kgrad, owned_vgrad], 0) * math.sqrt(groups * peer_count)
    stacked = jnp.stack([grad_query, grad_key, grad_value], 0).transpose(2, 0, 1, 3)
    stacked = stacked.reshape(row_count, 3 * number * HD).astype(jnp.bfloat16)
    grad_rows = jnp.einsum(
        "qc,dc->qd", stacked, qkv_weight, preferred_element_type=jnp.float32
    ).astype(jnp.bfloat16)
    back_rows = grad_rows[slot_index].reshape(peer_count, portion, features)
    returned = lax.all_to_all(back_rows, "ctx", split_axis=0, concat_axis=0, tiled=True)
    tile_grads = (
        jnp.zeros((row_count, features), jnp.bfloat16)
        .at[ordering]
        .set(returned.reshape(row_count, features))
    )
    return (tile_grads[None], weight_grad, far_pair[None])


def solution(mesh):
    placed = (
        P("slide", "ctx", None),
        P("slide", "ctx"),
        P("slide"),
        P(),
        P(),
        P("slide", "ctx", None),
    )
    return jax.shard_map(
        local,
        mesh=mesh,
        in_specs=placed,
        out_specs=(
            P("slide", "ctx", None),
            P(("slide", "ctx")),
            P("slide", None, None, "ctx", None),
        ),
        check_vma=False,
    )
```

profile of v0, /device:TPU:1, one launch (start us, length us, event | category | flops | bytes accessed | tf_op | source)
XLA Modules:
  0.0 295.0 jit_solution(11221221475237008115)
XLA Ops:
  8.8 3.8 %sort.17 = (s32[512]{0:T(512)}, s32[512]{0:T(512)S(1)}) sort(s32[512]{0:T(512)S(1)} %add_select_fusion.1, s32[512]{0:T(512)S(1)} %iota.79), dimensions={0}, to_apply=%region_0.1 | sort | flops 4608 | bytes 8192 | tf_op jit(solution)/shard_map/jit(argsort)/sort | solution.py:58
  12.6 3.6 %gather_fusion = s32[512]{0:T(512)S(1)} fusion(s32[512]{0:T(512)} %bitcast.162, s32[1024]{0:T(1024)S(1)} %pad_clamp_fusion.1), kind=kCustom, calls=%fused_computation | custom fusion | bytes 6144 | tf_op jit(solution)/shard_map/gather | solution.py:60
  16.9 5.2 %all-to-all-start = ((s32[8,1,64]{2,1,0:T(1,128)}), s32[8,1,64]{2,1,0:T(1,128)S(1)}, u32[]{:S(2)}, u32[]{:S(2)}) async-start(s32[8,1,64]{2,1,0:T(1,128)} %all_to_all.12), calls=%async_computation | async-start | bytes 8192 | tf_op jit(solution)/shard_map/all_to_all | solution.py:63
  22.9 1.9 convolution_convert_fusion.2
  25.7 2.8 copy.97
  28.5 2.4 select_reduce_fusion
  31.6 2.7 gather_fusion.1
  34.3 4.2 %all-to-all-start.1 = ((bf16[8,64,768]{2,1,0:T(8,128)(2,1)}), bf16[8,64,768]{2,1,0:T(8,128)(2,1)S(1)}, u32[]{:S(2)}, u32[]{:S(2)}) async-start(bf16[8,64,768]{2,1,0:T(8,128)(2,1)} %bitcast.174), calls=%async_computation.1 | async-start | bytes 1572864 | tf_op jit(solution)/shard_map/all_to_all | solution.py:62
  40.5 7.1 %all-to-all-done.1 = bf16[8,64,768]{2,1,0:T(8,128)(2,1)S(1)} async-done(((bf16[8,64,768]{2,1,0:T(8,128)(2,1)}), bf16[8,64,768]{2,1,0:T(8,128)(2,1)S(1)}, u32[]{:S(2)}, u32[]{:S(2)}) %all-to-all-start.1) | async-done | bytes 786464 | tf_op jit(solution)/shard_map/all_to_all | solution.py:62
  47.6 3.6 %scatter_custom_fusion = bf16[512,768]{1,0:T(8,128)(2,1)} fusion(s32[512]{0:T(512)S(1)} %bitcast.191, bf16[512,768]{1,0:T(8,128)(2,1)S(1)} %bitcast.181, bf16[]{:T(256)} %constant.16.clone.1), kind=kCustom, calls=%fused_computation.53 | custom fusion | bytes 786434 | tf_op jit(solution)/shard_map/scatter | solution.py:69
  51.2 3.3 %convolution_convert_fusion = bf16[512,1152]{1,0:T(8,128)(2,1)} fusion(bf16[512,768]{1,0:T(8,128)(2,1)} %scatter_custom_fusion, bf16[768,1152]{1,0:T(8,128)(2,1)S(1)} %copy-done), kind=kOutput, calls=%fused_computation.14 | convolution fusion | flops 906559488 | bytes 3735552 | tf_op jit(solution)/shard_map/dot_general | solution.py:71
  54.5 1.6 copy.71
  56.1 4.1 %fusion = (f32[6,512]{1,0:T(8,128)S(1)}, f32[6,512,512]{1,2,0:T(8,128)}) fusion(pred[512]{0:T(512)(128)(4,1)S(1)} %add_compare_fusion.2, bf16[512,3,6,64]{0,3,2,1:T(8,128)(2,1)S(1)} %bitcast.164), kind=kOutput, calls=%fused_computation.8 | convolution fusion | flops 206042112 | bytes 7090688 | tf_op jit(solution)/shard_map/qhd,khd->hqk/dot_general | solution.py:81
  61.2 2.2 copy.72
  67.4 12.1 %all_gather.6 = bf16[6,256,64]{2,1,0:T(8,128)(2,1)S(1)} all-gather(bf16[6,32,64]{2,1,0:T(8,128)(2,1)S(1)} %constant_dynamic-update-slice_fusion.6), channel_id=1, replica_groups=mesh['slide'=4,'ctx'=8] {'ctx'}, dimensions={1}, use_global_device_ids=true | all-gather | bytes 221184 | tf_op jit(solution)/shard_map/all_gather | solution.py:89
  84.9 1.6 broadcast_in_dim.305
  91.1 1.6 broadcast_in_dim.313
  94.0 4.5 %fusion.73 = f32[6,512]{1,0:T(8,128)S(1)} fusion(f32[6,512]{1,0:T(8,128)S(1)} %select_maximum_fusion, f32[6,512,512]{1,2,0:T(8,128)} %get-tuple-element.31, pred[512]{0:T(512)(128)(4,1)} %copy-done.27), kind=kLoop, calls=%fused_computation.139 | loop fusion | flops 7861248 | bytes 6316544 | tf_op jit(solution)/shard_map/reduce_sum | solution.py:107
  99.2 1.3 add_select_fusion
  100.6 2.2 copy.87
  103.9 9.5 %all_gather.7 = bf16[6,256,64]{2,1,0:T(8,128)(2,1)S(1)} all-gather(bf16[6,32,64]{2,1,0:T(8,128)(2,1)S(1)} %constant_dynamic-update-slice_fusion.12), channel_id=1, replica_groups=mesh['slide'=4,'ctx'=8] {'ctx'}, dimensions={1}, use_global_device_ids=true | all-gather | bytes 221184 | tf_op jit(solution)/shard_map/all_gather | solution.py:90
  115.1 1.3 broadcast_in_dim.320
  116.4 2.7 copy.94
  119.1 6.2 %fusion.75 = (bf16[6,512,64]{1,2,0:T(8,128)(2,1)}, f32[6,512]{1,0:T(8,128)}) fusion(bf16[512,6,64]{0,2,1:T(8,128)(2,1)} %bitcast.187, pred[512]{0:T(512)(128)(4,1)S(1)} %copy-done.28, f32[6,512]{1,0:T(8,128)} %add_select_fusion, f32[6,512,64]{1,2,0:T(8,128)} %copy.94, pred[6,512]{1,0:T(8,128)(4,1)S(1)} %copy-done.13, f32[6,512]{1,0:T(8,128)} %copy-done.14, ...), kind=kOutput, calls=%fused_computation.141 | convolution fusion | flops 210957312 | bytes 8300032 | tf_op jit(solution)/shard_map/hqk,khd->hqd/dot_general | solution.py:108
  125.3 1.4 reshape.241
  126.8 6.4 %multiply_convert_fusion = bf16[6,512,512]{1,2,0:T(8,128)(2,1)} fusion(f32[6,512]{1,0:T(8,128)} %get-tuple-element.11, f32[6,512]{1,0:T(8,128)} %add_select_fusion, bf16[512,6,64]{0,2,1:T(8,128)(2,1)} %bitcast.188, pred[512]{0:T(512)(128)(4,1)S(1)} %copy-done.28, bf16[512,3,6,64]{0,3,2,1:T(8,128)(2,1)S(1)} %bitcast.167, f32[6,512]{1,0:T(8,128)} %copy-done.14, ...), kind=kOutput, calls=%fused_computation.5 | convolution fusion | flops 215678976 | bytes 10261504 | tf_op jit(solution)/shard_map/hqd,khd->hqk/dot_general | solution.py:141
  134.0 1.4 fusion.53
  135.4 1.2 fusion.30
  137.5 1.3 broadcast_in_dim.327
  138.8 2.8 copy.98
  141.6 2.0 fusion.81
  143.9 2.6 convolution_multiply_fusion
  146.5 2.3 reshape.244
  148.9 2.7 fusion.22
  151.6 18.7 %reduce-scatter.5.cloned.1.call-done = f32[6,32,64]{2,1,0:T(8,128)} async-done(((f32[6,256,64]{2,1,0:T(8,128)}), f32[6,32,64]{2,1,0:T(8,128)}) %reduce-scatter.5.cloned.1.call-update) | async-done | bytes 49168 | tf_op jit(solution)/shard_map/reduce_scatter | solution.py:173
  170.3 2.2 broadcast_in_dim.331
  172.5 2.7 copy.102
  175.3 6.0 %fusion.24 = bf16[1,6,512,64]{2,3,1,0:T(8,128)(2,1)} fusion(f32[6,512]{1,0:T(8,128)S(1)} %copy-done.22, f32[6,512,64]{1,2,0:T(8,128)} %copy.102, pred[6,512]{1,0:T(8,128)(4,1)S(1)} %copy-done.13, bf16[512,6,64]{0,2,1:T(8,128)(2,1)} %bitcast.189, pred[512]{0:T(512)(128)(4,1)S(1)} %copy-done.29, f32[6,512,512]{1,2,0:T(8,128)} %get-tuple-element.31, ...), kind=kOutput, calls=%fused_computation.30 | convolution fusion | flops 211550208 | bytes 7892480 | tf_op jit(solution)/shard_map/hqk,hqd->hkd/dot_general | solution.py:149
  181.3 27.4 %reduce-scatter.3.cloned.1.call-done = f32[6,32,64]{2,1,0:T(8,128)} async-done(((f32[6,256,64]{2,1,0:T(8,128)}), f32[6,32,64]{2,1,0:T(8,128)}) %reduce-scatter.3.cloned.1.call-update) | async-done | bytes 49168 | tf_op jit(solution)/shard_map/reduce_scatter | solution.py:172
  208.7 2.2 broadcast_in_dim.329
  210.8 2.7 copy.100
  213.6 3.2 %fusion.23 = bf16[1,6,512,64]{2,3,1,0:T(8,128)(2,1)S(1)} fusion(bf16[6,512,512]{1,2,0:T(8,128)(2,1)} %multiply_convert_fusion, f32[6,512,64]{1,2,0:T(8,128)} %copy.100, pred[6,512]{1,0:T(8,128)(4,1)S(1)} %copy-done.13, bf16[512,3,6,64]{0,3,2,1:T(8,128)(2,1)S(1)} %bitcast.169), kind=kOutput, calls=%fused_computation.29 | convolution fusion | flops 201916416 | bytes 4722688 | tf_op jit(solution)/shard_map/hqk,qhd->hkd/dot_general | solution.py:148
  216.9 1.3 convolution_convert_fusion.1
  218.3 2.7 gather_fusion.2
  221.0 4.3 %all-to-all-start.2 = ((bf16[8,64,768]{2,1,0:T(8,128)(2,1)}), bf16[8,64,768]{2,1,0:T(8,128)(2,1)S(1)}, u32[]{:S(2)}, u32[]{:S(2)}) async-start(bf16[8,64,768]{2,1,0:T(8,128)(2,1)} %bitcast.175), calls=%async_computation.4 | async-start | bytes 1572864 | tf_op jit(solution)/shard_map/all_to_all | solution.py:184
  225.3 56.5 %all-reduce.3.cloned.1.call-done = f32[294912]{0:T(1024)} async-done(((f32[294912]{0:T(1024)}), f32[294912]{0:T(1024)}) %all-reduce.3.cloned.1.call-update) | async-done | bytes 1179664
  281.8 1.4 dynamic-slice
  283.9 3.7 %scatter_custom_fusion.1 = bf16[512,768]{1,0:T(8,128)(2,1)} fusion(s32[512]{0:T(512)} %copy-done.30, bf16[512,768]{1,0:T(8,128)(2,1)S(1)} %bitcast.180, bf16[]{:T(256)} %constant.16.clone.1), kind=kCustom, calls=%fused_computation.51 | custom fusion | bytes 786944 | tf_op jit(solution)/shard_map/scatter | solution.py:188
  (123 shorter events, 27.9 us)
Async XLA Ops:
  8.0 43.2 %copy-start = (bf16[768,1152]{1,0:T(8,128)(2,1)S(1)}, bf16[768,1152]{1,0:T(8,128)(2,1)}, u32[]{:S(2)}) copy-start(bf16[768,1152]{1,0:T(8,128)(2,1)} %param.9) | copy-start | bytes 5308420
  12.6 10.2 %copy-start.30 = (s32[512]{0:T(512)}, s32[512]{0:T(512)S(1)}, u32[]{:S(2)}) copy-start(s32[512]{0:T(512)S(1)} %compare_select_fusion.1) | copy-start | bytes 6148
  16.9 17.4 %all-to-all-start = ((s32[8,1,64]{2,1,0:T(1,128)}), s32[8,1,64]{2,1,0:T(1,128)S(1)}, u32[]{:S(2)}, u32[]{:S(2)}) async-start(s32[8,1,64]{2,1,0:T(1,128)} %all_to_all.12), calls=%async_computation | async-start | bytes 8192 | tf_op jit(solution)/shard_map/all_to_all | solution.py:63
  22.2 16.3 %copy-start.24 = (pred[6,16]{1,0:T(8,128)(4,1)}, pred[6,16]{1,0:T(8,128)(4,1)S(1)}, u32[]{:S(2)}) copy-start(pred[6,16]{1,0:T(8,128)(4,1)S(1)} %iota_compare_fusion) | copy-start | bytes 292
  22.8 33.2 %copy-start.27 = (pred[512]{0:T(512)(128)(4,1)}, pred[512]{0:T(512)(128)(4,1)S(1)}, u32[]{:S(2)}) copy-start(pred[512]{0:T(512)(128)(4,1)S(1)} %add_compare_fusion.2) | copy-start | bytes 1540
  22.8 8.7 %copy-start.1 = (bf16[1,512,768]{2,1,0:T(8,128)(2,1)S(1)}, bf16[1,512,768]{2,1,0:T(8,128)(2,1)}, u32[]{:S(2)}) copy-start(bf16[1,512,768]{2,1,0:T(8,128)(2,1)} %param.6) | copy-start | bytes 2359300
  24.7 9.5 %copy-start.11 = (bf16[512,384]{0,1:T(8,128)(2,1)}, bf16[512,384]{0,1:T(8,128)(2,1)S(1)}, u32[]{:S(2)}) copy-start(bf16[512,384]{0,1:T(8,128)(2,1)S(1)} %convolution_convert_fusion.2) | copy-start | bytes 1179652
  34.3 13.3 %all-to-all-start.1 = ((bf16[8,64,768]{2,1,0:T(8,128)(2,1)}), bf16[8,64,768]{2,1,0:T(8,128)(2,1)S(1)}, u32[]{:S(2)}, u32[]{:S(2)}) async-start(bf16[8,64,768]{2,1,0:T(8,128)(2,1)} %bitcast.174), calls=%async_computation.1 | async-start | bytes 1572864 | tf_op jit(solution)/shard_map/all_to_all | solution.py:62
  38.5 131.9 %reduce-scatter.5.cloned.1.call-start = ((), (), s32[]{:S(2)}) async-start(), calls=%async_computation.6 | async-start | bytes 884736 | tf_op jit(solution)/shard_map/reduce_scatter | solution.py:173
  83.6 0.6 copy-start.19
  88.3 0.6 copy-start.16
  89.8 0.6 copy-start.20
  93.4 0.6 copy-start.14
  100.6 18.6 %copy-start.13 = (pred[6,512]{1,0:T(8,128)(4,1)S(1)}, pred[6,512]{1,0:T(8,128)(4,1)}, u32[]{:S(2)}) copy-start(pred[6,512]{1,0:T(8,128)(4,1)} %broadcast_in_dim.301) | copy-start | bytes 9220
  100.6 18.6 %copy-start.28 = (pred[512]{0:T(512)(128)(4,1)S(1)}, pred[512]{0:T(512)(128)(4,1)}, u32[]{:S(2)}) copy-start(pred[512]{0:T(512)(128)(4,1)} %copy-done.27) | copy-start | bytes 1540
  113.4 0.8 copy-start.2
  126.8 6.4 %copy-start.9 = (f32[6,32,16]{2,1,0:T(8,128)S(1)}, f32[6,32,16]{2,1,0:T(8,128)}, u32[]{:S(2)}) copy-start(f32[6,32,16]{2,1,0:T(8,128)} %reduce_sum.69) | copy-start | bytes 36868
  126.8 6.4 %copy-start.10 = (f32[6,32,16]{2,1,0:T(8,128)S(1)}, f32[6,32,16]{2,1,0:T(8,128)}, u32[]{:S(2)}) copy-start(f32[6,32,16]{2,1,0:T(8,128)} %reshape.241) | copy-start | bytes 36868
  126.8 6.4 %copy-start.21 = (f32[6,32]{1,0:T(8,128)S(1)}, f32[6,32]{1,0:T(8,128)}, u32[]{:S(2)}) copy-start(f32[6,32]{1,0:T(8,128)} %copy-done.20) | copy-start | bytes 2308
  126.8 6.4 %copy-start.23 = (pred[32,16]{1,0:T(8,128)(4,1)S(1)}, pred[32,16]{1,0:T(8,128)(4,1)}, u32[]{:S(2)}) copy-start(pred[32,16]{1,0:T(8,128)(4,1)} %add_compare_fusion) | copy-start | bytes 1540
  126.8 6.4 %copy-start.25 = (pred[6,16]{1,0:T(8,128)(4,1)S(1)}, pred[6,16]{1,0:T(8,128)(4,1)}, u32[]{:S(2)}) copy-start(pred[6,16]{1,0:T(8,128)(4,1)} %copy-done.24) | copy-start | bytes 292
  126.8 7.2 %copy-start.12 = (bf16[6,32,64]{2,1,0:T(8,128)(2,1)S(1)}, bf16[6,32,64]{2,1,0:T(8,128)(2,1)}, u32[]{:S(2)}) copy-start(bf16[6,32,64]{2,1,0:T(8,128)(2,1)} %select_reduce_fusion) | copy-start | bytes 73732
  126.8 7.2 %copy-start.17 = (f32[6,32]{1,0:T(8,128)S(1)}, f32[6,32]{1,0:T(8,128)}, u32[]{:S(2)}) copy-start(f32[6,32]{1,0:T(8,128)} %copy-done.16) | copy-start | bytes 2308
  126.8 7.2 %copy-start.18 = (pred[6,256]{1,0:T(8,128)(4,1)S(1)}, pred[6,256]{1,0:T(8,128)(4,1)}, u32[]{:S(2)}) copy-start(pred[6,256]{1,0:T(8,128)(4,1)} %add_compare_fusion.1) | copy-start | bytes 4612
  135.4 73.3 %reduce-scatter.3.cloned.1.call-start = ((), (), s32[]{:S(2)}) async-start(), calls=%async_computation.5 | async-start | bytes 884736 | tf_op jit(solution)/shard_map/reduce_scatter | solution.py:172
  136.7 0.6 copy-start.5
  137.5 4.1 %copy-start.6 = (bf16[6,32,256]{2,1,0:T(8,128)(2,1)S(1)}, bf16[6,32,256]{2,1,0:T(8,128)(2,1)}, u32[]{:S(2)}) copy-start(bf16[6,32,256]{2,1,0:T(8,128)(2,1)} %copy-done.5) | copy-start | bytes 294916
  137.5 6.3 %copy-start.3 = (bf16[6,512,64]{1,2,0:T(8,128)(2,1)S(1)}, bf16[6,512,64]{1,2,0:T(8,128)(2,1)}, u32[]{:S(2)}) copy-start(bf16[6,512,64]{1,2,0:T(8,128)(2,1)} %get-tuple-element.10) | copy-start | bytes 1179652
  143.6 138.2 %all-reduce.3.cloned.1.call-start = ((), (), s32[]{:S(2)}) async-start(), calls=%async_computation.7 | async-start | bytes 2359296
  151.6 23.7 %copy-start.15 = (f32[6,512]{1,0:T(8,128)S(1)}, f32[6,512]{1,0:T(8,128)}, u32[]{:S(2)}) copy-start(f32[6,512]{1,0:T(8,128)} %copy-done.14) | copy-start | bytes 36868
  151.6 23.7 %copy-start.22 = (f32[6,512]{1,0:T(8,128)S(1)}, f32[6,512]{1,0:T(8,128)}, u32[]{:S(2)}) copy-start(f32[6,512]{1,0:T(8,128)} %add_select_fusion) | copy-start | bytes 36868
  151.6 23.7 %copy-start.29 = (pred[512]{0:T(512)(128)(4,1)S(1)}, pred[512]{0:T(512)(128)(4,1)}, u32[]{:S(2)}) copy-start(pred[512]{0:T(512)(128)(4,1)} %copy-done.27) | copy-start | bytes 1540
  213.6 3.2 %copy-start.4 = (bf16[1,6,512,64]{2,3,1,0:T(8,128)(2,1)S(1)}, bf16[1,6,512,64]{2,3,1,0:T(8,128)(2,1)}, u32[]{:S(2)}) copy-start(bf16[1,6,512,64]{2,3,1,0:T(8,128)(2,1)} %fusion.24) | copy-start | bytes 1179652
  216.9 1.3 copy-start.26
  218.2 65.0 %copy-start.7 = (f32[6,32,64]{2,1,0:T(8,128)S(1)}, f32[6,32,64]{2,1,0:T(8,128)}, u32[]{:S(2)}) copy-start(f32[6,32,64]{2,1,0:T(8,128)} %reduce-scatter.5.cloned.1.call-done) | copy-start | bytes 147460
  218.2 65.0 %copy-start.8 = (f32[6,32,64]{2,1,0:T(8,128)S(1)}, f32[6,32,64]{2,1,0:T(8,128)}, u32[]{:S(2)}) copy-start(f32[6,32,64]{2,1,0:T(8,128)} %reduce-scatter.3.cloned.1.call-done) | copy-start | bytes 147460
  221.0 62.9 %all-to-all-start.2 = ((bf16[8,64,768]{2,1,0:T(8,128)(2,1)}), bf16[8,64,768]{2,1,0:T(8,128)(2,1)S(1)}, u32[]{:S(2)}, u32[]{:S(2)}) async-start(bf16[8,64,768]{2,1,0:T(8,128)(2,1)} %bitcast.175), calls=%async_computation.4 | async-start | bytes 1572864 | tf_op jit(solution)/shard_map/all_to_all | solution.py:184
Sparse Core Ops, SparseCore 0:
  135.5 34.7 reduce-scatter.4
  173.5 35.1 reduce-scatter.2
Sparse Core Ops, SparseCore 1:
  151.7 130.0 all-reduce.2
where the time goes:
time: 298 us; the launch traced here: 295 us
  waiting for transfers between devices  110 us (37%)
  local copies, waits for them, and re-layouts  68.5 us (23%)
  matrix products  44.5 us (15%)
  blocking collectives  21.7 us (7%)
  other arithmetic  19.9 us (7%)
  between operations  16.6 us (6%)
  starting transfers between devices  14.1 us (5%)
    unnamed x4, waiting for transfers between devices  56.6 us
    reduce_scatter x1, waiting for transfers between devices, local(): lax.psum_scatter(partial_keys, 'ctx', scatter_dimension=1, tiled=True)  27.4 us
    reduce_scatter x1, waiting for transfers between devices, local(): lax.psum_scatter(partial_values, 'ctx', scatter_dimension=1, tiled=True)  18.7 us
    broadcast_in_dim x8, local copies, waits for them, and re-layouts, spread_rows(): placed = jnp.where(chosen[:, None, :, None], values[:, :, None, :], 0.0)  17.8 us
    all_gather x1, blocking collectives, local(): lax.all_gather(near_keys, 'ctx', axis=1, tiled=True)  12.1 us
    all_gather x1, blocking collectives, local(): lax.all_gather(near_values, 'ctx', axis=1, tiled=True)  9.54 us
    unnamed x78, local copies, waits for them, and re-layouts  8.34 us
    all_to_all x1, waiting for transfers between devices, local(): lax.all_to_all(sent_rows, 'ctx', split_axis=0, concat_axis=0, tiled=True)  7.09 us
  transfers between devices with their start and end apart: 6, of which 4 were waited for; matrix products, arithmetic and copies ran while one was open for 18% of the time, Pallas kernels for 0%

commit v1 on v0

v1 whole, which is shorter than its diff:
```python
import functools
import math

import jax
import jax.numpy as jnp
from jax import lax
from jax.experimental import pallas as pl
from jax.experimental.pallas import tpu as pltpu
from jax.sharding import PartitionSpec as P

HD = 64
STRIDE = 16
FLOOR = -1e30
BF = jnp.bfloat16
F32 = jnp.float32
HIGH = lax.Precision.HIGHEST
MESH = pl.DeviceIdType.MESH


def dot(a, b):
    return lax.dot_general(a, b, (((1,), (0,)), ((), ())), preferred_element_type=F32)


def dot_t(a, b):
    return lax.dot_general(a, b, (((1,), (1,)), ((), ())), preferred_element_type=F32)


def exact_dot(a, b, last):
    return lax.dot_general(
        a, b, (((1,), (last,)), ((), ())), precision=HIGH, preferred_element_type=F32
    )


def flip(x):
    return x.astype(F32).T.astype(BF)


def halves(x):
    high = x.astype(BF)
    return high, (x - high.astype(F32)).astype(BF)


def iota(shape, dim):
    return lax.broadcasted_iota(jnp.int32, shape, dim)


def hot(cond):
    return jnp.where(cond, 1.0, 0.0).astype(BF)


def column(row):
    return jnp.broadcast_to(row, (128, row.shape[1])).T[:, :1]


def layer(n, slides, fused, len_ref, pos_ref, tiles_ref, wqkv_ref, wout_ref, cot_ref,
          grads_ref, wgrad_ref, far_ref,
          sent, psend, got, pbuf, slot_ref, st_ref, rt_ref, proj, g_ref, gt_ref, kt_ref, vt_ref,
          w_ref, dp_ref, m_ref, l_ref, nt_ref, att_ref, stat_ref, fbuf, gbuf, stats, sbuf,
          dqt_ref, dk_ref, dv_ref, bsend, bbuf, pw, wbuf, zs, zbuf,
          send_sems, recv_sems, zsend, zrecv):
    me = lax.axis_index("ctx")
    my_slide = lax.axis_index("slide")
    t, d = tiles_ref.shape
    hc = wout_ref.shape[0]
    heads = hc // HD
    portion = t // n
    g = t // STRIDE
    fq = heads * g
    nf = n * g

    barrier = pltpu.get_barrier_semaphore()

    def greet(k, carry):
        pl.semaphore_signal(barrier, inc=1, device_id={"ctx": lax.rem(me + k, n)},
                            device_id_type=MESH)
        return carry

    lax.fori_loop(1, n, greet, 0)
    if fused:
        for k in range(1, slides):
            pl.semaphore_signal(barrier, inc=1,
                                device_id={"slide": lax.rem(my_slide + k, slides)},
                                device_id_type=MESH)

    def copy_to(which, k, src, dst):
        return pltpu.make_async_remote_copy(
            src_ref=src, dst_ref=dst, send_sem=send_sems.at[which, k],
            recv_sem=recv_sems.at[which, k], device_id={"ctx": lax.rem(me + k, n)},
            device_id_type=MESH)

    def push(which, source, target):
        def body(k, carry):
            copy_to(which, k, source(lax.rem(me + k, n)), target.at[me]).start()
            return carry
        lax.fori_loop(1, n, body, 0)

    def landed(which, target):
        def body(k, carry):
            owner = lax.rem(me + n - k, n)
            copy_to(which, k, target.at[owner], target.at[owner]).wait_recv()
            return carry
        lax.fori_loop(1, n, body, 0)

    def left(which, target):
        def body(k, carry):
            copy_to(which, k, target.at[0], target.at[0]).wait_send()
            return carry
        lax.fori_loop(1, n, body, 0)

    length = len_ref[0]

    prow = pos_ref[...].astype(F32)
    pcol = column(prow)
    rank = jnp.sum(jnp.where(pcol < prow, 1.0, 0.0), axis=0, keepdims=True)
    down = iota((t, t), 0).astype(F32)
    across = iota((t, t), 1).astype(F32)
    sent[...] = dot(hot(rank == down), tiles_ref[...]).astype(BF).reshape(n, portion, d)
    placed = column(rank) == across
    st_ref[...] = hot(placed)
    ordered = jnp.sum(jnp.where(placed, pcol, 0.0), axis=0, keepdims=True)
    psend[...] = jnp.zeros_like(psend)
    for k in range(n):
        psend[k, :, 0:portion] = jnp.broadcast_to(
            ordered[:, k * portion:(k + 1) * portion], (8, portion))
    pl.semaphore_wait(barrier, n - 1 + (slides - 1 if fused else 0))
    push(1, lambda peer: psend.at[peer], pbuf)
    push(0, lambda peer: sent.at[peer], got)
    got[me] = sent[me]
    pbuf[me] = psend[me]

    base = me * t
    live_row = base + iota((1, t), 1) < length
    live_col = base + iota((t, 1), 0) < length
    grad_rows = jnp.where(live_col, dot_t(cot_ref[...], wout_ref[...]), 0.0)
    g_ref[...] = grad_rows.astype(BF)
    gt_ref[...] = jnp.where(live_row, dot_t(wout_ref[...], cot_ref[...]), 0.0).astype(BF)
    gather = hot(iota((g, t), 1) // STRIDE == iota((g, t), 0))
    own_head = iota((t, hc), 0) % STRIDE == iota((t, hc), 1) // HD
    gbuf[me] = dot(gather, jnp.where(own_head, grad_rows, 0.0).astype(BF)).astype(BF)
    push(2, lambda peer: gbuf.at[me], gbuf)

    landed(1, pbuf)
    for k in range(n):
        slot_ref[:, k * portion:(k + 1) * portion] = pbuf[k, :, 0:portion]
    slot = slot_ref[0:1, :] - (me * t).astype(F32)
    rt_ref[...] = hot(column(slot) == across)
    put = hot(slot == down)
    landed(0, got)
    sequence = dot(put, got[...].reshape(t, d)).astype(BF)
    for k in range(3):
        cols = slice(k * hc, (k + 1) * hc)
        part = dot(sequence, wqkv_ref[:, cols])
        rounded = part.astype(BF)
        proj[:, cols] = rounded
        fbuf[me, :, cols] = dot(gather, jnp.where(own_head, part, 0.0).astype(BF)).astype(BF)
        if k == 1:
            kt_ref[...] = flip(rounded)
        if k == 2:
            vt_ref[...] = flip(rounded)
    push(3, lambda peer: fbuf.at[me], fbuf)

    m_ref[...] = jnp.zeros_like(m_ref)
    l_ref[...] = jnp.zeros_like(l_ref)
    stat_ref[...] = jnp.zeros_like(stat_ref)
    lane = iota((1, 2 * HD), 1)

    for pair in range(heads // 2):
        cols = slice(pair * 128, pair * 128 + 128)
        q2 = proj[:, cols]
        k2 = proj[:, hc + pair * 128:hc + pair * 128 + 128]
        v2 = proj[:, 2 * hc + pair * 128:2 * hc + pair * 128 + 128]
        for half in range(2):
            h = 2 * pair + half
            rows = slice(h * HD, h * HD + HD)
            mine = hot(lane // HD == half)
            score = jnp.where(live_col, dot_t(k2 * mine, q2) * 0.125, FLOOR)
            top = jnp.max(score, axis=0, keepdims=True)
            weight = jnp.where(live_col, jnp.exp(score - top), 0.0)
            w_ref[h] = weight
            m_ref[h:h + 1, :] = top
            l_ref[h:h + 1, :] = jnp.sum(weight, axis=0, keepdims=True)
            nt_ref[rows, :] = dot(vt_ref[rows, :], weight.astype(BF))
            dp_ref[h] = dot(v2 * mine, gt_ref[cols, :])

    landed(2, gbuf)
    landed(3, fbuf)
    all_q = fbuf[:, :, 0:hc].reshape(nf, hc)
    all_k = fbuf[:, :, hc:2 * hc].reshape(nf, hc)
    all_v = fbuf[:, :, 2 * hc:3 * hc].reshape(nf, hc)
    all_g = gbuf[...].reshape(nf, hc)
    block = hot(iota((fq, hc), 0) // g == iota((fq, hc), 1) // HD)

    def diagonal(x):
        return jnp.concatenate([x] * heads, axis=0) * block

    own_q = diagonal(fbuf[me, :, 0:hc])
    own_k = diagonal(fbuf[me, :, hc:2 * hc])
    own_v = diagonal(fbuf[me, :, 2 * hc:3 * hc])
    own_g = diagonal(gbuf[me])
    place = iota((fq, t), 1) == (iota((fq, t), 0) % g) * STRIDE + iota((fq, t), 0) // g
    spread = jnp.where(place, 1.0, 0.0)
    spread_bf = spread.astype(BF)
    head_rows = iota((8, fq), 0) == iota((8, fq), 1) // g

    def widen(row):
        return exact_dot(jnp.where(head_rows, row, 0.0), spread, 0)

    def narrow(rows):
        return jnp.sum(jnp.where(head_rows, exact_dot(rows, spread, 1), 0.0), axis=0,
                       keepdims=True)

    def spread_cols(x):
        kept = jnp.where(iota((hc, fq), 0) // HD == iota((hc, fq), 1) // g, x, 0.0)
        high, low = halves(kept)
        return dot(high, spread_bf) + dot(low, spread_bf)

    far_live = iota((nf, fq), 0) * STRIDE + iota((nf, fq), 1) // g < length
    far_score = jnp.where(far_live, dot_t(all_k, own_q) * 0.125, FLOOR)
    far_top = jnp.max(far_score, axis=0, keepdims=True)
    chosen = iota((8, t), 1) % STRIDE == iota((8, t), 0)
    tops = m_ref[...]
    ceiling = jnp.maximum(tops, jnp.where(chosen, widen(far_top), FLOOR))
    rescale = jnp.exp(tops - ceiling)
    far_weight = jnp.where(far_live, jnp.exp(far_score - narrow(ceiling)), 0.0)
    totals = l_ref[...] * rescale + widen(jnp.sum(far_weight, axis=0, keepdims=True))
    inverse = 1.0 / jnp.where(live_row, totals, 1.0)
    inverse = jnp.where(iota((8, t), 0) < heads, inverse, 0.0)
    far_numer = spread_cols(dot(flip(all_v), far_weight.astype(BF)))
    for h in range(heads):
        rows = slice(h * HD, h * HD + HD)
        result = (nt_ref[rows, :] * rescale[h:h + 1] + far_numer[rows, :]) * inverse[h:h + 1]
        result = jnp.where(live_row, result, 0.0)
        att_ref[rows, :] = result.astype(BF)
        stat_ref[h:h + 1, :] = jnp.sum(gt_ref[rows, :].astype(F32) * result, axis=0, keepdims=True)
    stat = stat_ref[...]

    stats[...] = jnp.zeros_like(stats)
    stats[0:8, :] = ceiling
    stats[8:16, :] = inverse
    stats[16:24, :] = stat
    turned = stats[...].T
    wanted = iota((t, 128), 0) % STRIDE == iota((t, 128), 1) % 8
    sbuf[me] = jnp.sum(jnp.where(wanted, turned, 0.0).reshape(g, STRIDE, 128), axis=1)
    push(4, lambda peer: sbuf.at[me], sbuf)

    factor = 1.0 / math.sqrt(slides * n * t)
    if fused:
        run = hc // (n * slides)
        spot = iota((hc, hc), 0)
        source = (spot % (run * slides)) // run * (n * run) + spot // (run * slides) * run + spot % run
        order = hot(iota((hc, hc), 1) == source)
        att = dot(order, att_ref[...]).astype(BF)
        pw[...] = (dot(att, cot_ref[...]) * factor).astype(BF).reshape(n, hc // n, d)
        wbuf[me] = pw[me]
        push(5, lambda peer: pw.at[peer], wbuf)
    else:
        wgrad_ref[...] = dot(att_ref[...], cot_ref[...]) * factor

    for pair in range(heads // 2):
        cols = slice(pair * 128, pair * 128 + 128)
        q2 = proj[:, cols]
        g2 = g_ref[:, cols]
        key_parts = []
        value_parts = []
        for half in range(2):
            h = 2 * pair + half
            rows = slice(h * HD, h * HD + HD)
            prob = w_ref[h] * (rescale[h:h + 1] * inverse[h:h + 1])
            dscore = (prob * (dp_ref[h] - stat[h:h + 1]) * 0.125).astype(BF)
            dqt_ref[rows, :] = dot(kt_ref[rows, :], dscore)
            key_parts.append(dot(dscore, q2))
            value_parts.append(dot(prob.astype(BF), g2))
        dk_ref[:, cols] = jnp.where(lane < HD, key_parts[0], key_parts[1])
        dv_ref[:, cols] = jnp.where(lane < HD, value_parts[0], value_parts[1])

    far_prob = far_weight * narrow(inverse)
    far_dscore = far_prob * (dot_t(all_v, own_g) - narrow(stat)) * 0.125
    dqt = dqt_ref[...] + spread_cols(dot(flip(all_k), far_dscore.astype(BF)))
    proj[:, 0:hc] = dqt.T.astype(BF)
    landed(4, sbuf)
    rows_all = sbuf[...].reshape(nf, 128).T

    def per_head(first):
        return jnp.concatenate(
            [jnp.broadcast_to(rows_all[first + h:first + h + 1], (g, nf)) for h in range(heads)], axis=0)

    key_spot = iota((fq, 1), 0)
    key_live = (me * g + key_spot % g) * STRIDE + key_spot // g < length
    own_score = dot_t(own_k, all_q) * 0.125
    own_weight = jnp.where(key_live, jnp.exp(jnp.where(key_live, own_score - per_head(0), 0.0)), 0.0)
    own_prob = own_weight * per_head(8)
    own_dscore = own_prob * (dot_t(own_v, all_g) - per_head(16)) * 0.125
    scale = math.sqrt(nf)
    back_spread = hot(iota((t, fq), 0)
                      == (iota((t, fq), 1) % g) * STRIDE + iota((t, fq), 1) // g)
    keep = iota((fq, hc), 0) // g == iota((fq, hc), 1) // HD
    for which, left_side, right_side, base_ref in (
        (0, own_dscore, all_q, dk_ref), (1, own_prob, all_g, dv_ref)
    ):
        term = dot(left_side.astype(BF), right_side)
        for h in range(heads):
            far_ref[which, h] = term[h * g:(h + 1) * g, h * HD:(h + 1) * HD] * scale
        high, low = halves(jnp.where(keep, term, 0.0))
        total = base_ref[...] + dot(back_spread, high) + dot(back_spread, low)
        proj[:, (which + 1) * hc:(which + 2) * hc] = total.astype(BF)

    grad_seq = dot_t(proj[...], wqkv_ref[...]).astype(BF)
    bsend[...] = dot(rt_ref[...], grad_seq).astype(BF).reshape(n, portion, d)
    push(6, lambda peer: bsend.at[peer], bbuf)
    bbuf[me] = bsend[me]

    if fused:
        def slide_copy(k, src, dst):
            return pltpu.make_async_remote_copy(
                src_ref=src, dst_ref=dst, send_sem=zsend.at[k], recv_sem=zrecv.at[k],
                device_id={"slide": lax.rem(my_slide + k, slides)}, device_id_type=MESH)

        landed(5, wbuf)
        summed = jnp.sum(wbuf[...].astype(F32), axis=0)
        zs[...] = jnp.zeros_like(zs)
        for k in range(slides):
            zs[k, 0:run, :] = summed[k * run:(k + 1) * run, :]
        for k in range(1, slides):
            slide_copy(k, zs.at[lax.rem(my_slide + k, slides)], zbuf.at[my_slide]).start()
        zbuf[my_slide] = zs[my_slide]

    landed(6, bbuf)
    grads_ref[...] = dot(st_ref[...], bbuf[...].reshape(t, d)).astype(BF)

    if fused:
        for k in range(1, slides):
            owner = lax.rem(my_slide + slides - k, slides)
            slide_copy(k, zbuf.at[owner], zbuf.at[owner]).wait_recv()
        wgrad_ref[...] = jnp.sum(zbuf[...], axis=0)[0:run, :]
        for k in range(1, slides):
            slide_copy(k, zs.at[0], zbuf.at[0]).wait_send()
        left(5, wbuf)
    for which, target in ((0, got), (1, pbuf), (2, gbuf), (3, fbuf), (4, sbuf), (6, bbuf)):
        left(which, target)


def local(slides, n, tiles, tile_pos, lengths, qkv_weight, out_weight, cotangent):
    _, t, d = tiles.shape
    hc = out_weight.shape[0]
    heads = hc // HD
    portion = t // n
    g = t // STRIDE
    fused = hc % (n * slides) == 0 and (hc // n) % 16 == 0
    run = hc // (n * slides) if fused else 0
    pad = -(-run // 8) * 8 if fused else 8
    wrows = hc // n if fused else 16
    vm = pltpu.VMEM
    scratch = [
        vm((n, portion, d), BF), vm((n, 8, 128), F32), vm((n, portion, d), BF),
        vm((n, 8, 128), F32), vm((8, t), F32), vm((t, t), BF), vm((t, t), BF),
        vm((t, 3 * hc), BF), vm((t, hc), BF), vm((hc, t), BF), vm((hc, t), BF), vm((hc, t), BF),
        vm((heads, t, t), F32), vm((heads, t, t), F32), vm((8, t), F32), vm((8, t), F32),
        vm((hc, t), F32), vm((hc, t), BF), vm((8, t), F32),
        vm((n, g, 3 * hc), BF), vm((n, g, hc), BF), vm((128, t), F32), vm((n, g, 128), F32),
        vm((hc, t), F32), vm((t, hc), F32), vm((t, hc), F32),
        vm((n, portion, d), BF), vm((n, portion, d), BF),
        vm((n, wrows, d), BF), vm((n, wrows, d), BF),
        vm((slides, pad, d), F32), vm((slides, pad, d), F32),
        pltpu.SemaphoreType.DMA((7, n)), pltpu.SemaphoreType.DMA((7, n)),
        pltpu.SemaphoreType.DMA((slides,)), pltpu.SemaphoreType.DMA((slides,)),
    ]
    spec = pl.BlockSpec(memory_space=pltpu.VMEM)
    grads, wgrad, far = pl.pallas_call(
        functools.partial(layer, n, slides, fused),
        out_shape=(
            jax.ShapeDtypeStruct((t, d), BF),
            jax.ShapeDtypeStruct((run if fused else hc, d), F32),
            jax.ShapeDtypeStruct((2, heads, g, HD), F32),
        ),
        in_specs=[pl.BlockSpec(memory_space=pltpu.SMEM)] + [spec] * 5,
        out_specs=(spec, spec, spec),
        scratch_shapes=scratch,
        compiler_params=pltpu.CompilerParams(
            collective_id=0, has_side_effects=True, vmem_limit_bytes=56 * 1024 * 1024
        ),
        cost_estimate=pl.CostEstimate(flops=8 * 10**9, bytes_accessed=6 * 10**6, transcendentals=2 * 10**6),
    )(lengths, tile_pos, tiles[0], qkv_weight, out_weight, cotangent[0])
    if fused:
        wgrad = wgrad.reshape(-1)
    else:
        wgrad = lax.psum_scatter(
            wgrad.reshape(-1), ("slide", "ctx"), scatter_dimension=0, tiled=True
        )
    return grads[None], wgrad, far[None]


def solution(mesh):
    placed = (
        P("slide", "ctx", None),
        P("slide", "ctx"),
        P("slide"),
        P(),
        P(),
        P("slide", "ctx", None),
    )
    return jax.shard_map(
        functools.partial(local, mesh.shape["slide"], mesh.shape["ctx"]),
        mesh=mesh,
        in_specs=placed,
        out_specs=(
            P("slide", "ctx", None),
            P(("slide", "ctx")),
            P("slide", None, None, "ctx", None),
        ),
        check_vma=False,
    )
```

time: 298 us -> 57.9 us (0.19)
  waiting for transfers between devices: 110 us -> 0 us
  local copies, waits for them, and re-layouts: 68.5 us -> 4.2 us
  Pallas kernels: 0 us -> 52.2 us
  matrix products: 44.5 us -> 0 us
  blocking collectives: 21.7 us -> 0 us
  other arithmetic: 19.9 us -> 0 us
  between operations: 16.6 us -> 1.29 us
  starting transfers between devices: 14.1 us -> 0 us
    unnamed x4 -> x0, waiting for transfers between devices: 56.6 us -> none
    pallas_call x0 -> x1, Pallas kernels: none -> 52.2 us  [local(): pl.pallas_call(functools.partial(layer, n, slides, fused), out_shape=(jax...]
    reduce_scatter x2 -> x0, waiting for transfers between devices: 46.1 us -> none  [the longest x1 27.4 us: local(): lax.psum_scatter(partial_keys, 'ctx', scatter_dimension=1, tiled=True)]
    dot_general x16 -> x0, matrix products: 44.5 us -> none  [the longest x1 6.36 us: local(): jnp.einsum('hqd,khd->hqk', grad_out, values, preferred_element_type=jnp.f...]
    broadcast_in_dim x14 -> x0, local copies, waits for them, and re-layouts: 23.2 us -> none  [the longest x8 17.8 us: spread_rows(): placed = jnp.where(chosen[:, None, :, None], values[:, :, None, :], 0.0)]
    all_gather x2 -> x0, blocking collectives: 21.7 us -> none  [the longest x1 12.1 us: local(): lax.all_gather(near_keys, 'ctx', axis=1, tiled=True)]
    all_to_all x3 -> x0, starting transfers between devices: 13.8 us -> none  [the longest x1 5.22 us: local(): lax.all_to_all(sent_places, 'ctx', split_axis=0, concat_axis=0, tiled=True)]
    slice x7 -> x0, local copies, waits for them, and re-layouts: 9.72 us -> none  [the longest x3 3.28 us: dilate(): lattice[:, offset, offset, :]]
  transfers between devices with their start and end apart: 6 -> 0, of which waited for: 4 -> 0; matrix products, arithmetic and copies ran while one was open for 18% -> 0% of each run, Pallas kernels for 0% -> 0%
where the time goes in v1:
time: 57.9 us; the launch traced here: 57.7 us
  Pallas kernels  52.2 us (90%)
  local copies, waits for them, and re-layouts  4.2 us (7%)
  between operations  1.29 us (2%)
    pallas_call x1, Pallas kernels, local(): pl.pallas_call(functools.partial(layer, n, slides, fused), out_shape=(jax...  52.2 us
    unnamed x4, local copies, waits for them, and re-layouts  2.74 us
    reshape x1, local copies, waits for them, and re-layouts, local(): wgrad = wgrad.reshape(-1)  1.46 us

profile of v1, /device:TPU:1, one launch (start us, length us, event | category | flops | bytes accessed | tf_op | source)
XLA Modules:
  0.0 57.7 jit_solution(6163295821418289716)
XLA Ops:
  1.3 52.2 %shard_map.85 = (bf16[512,768]{1,0:T(8,128)(2,1)}, f32[12,768]{1,0:T(8,128)}, f32[2,6,32,64]{3,2,1,0:T(8,128)}) custom-call(s32[1]{0:T(128)S(6)} %copy.11.len_ref, s32[1,512]{1,0:T(1,128)} %pos_ref.1, bf16[512,768]{1,0:T(8,128)(2,1)} %bitcast.6, bf16[768,1152]{1,0:T(8,128)(2,1)} %wqkv_ref.1, bf16[384,768]{1,0:T(8,128)(2,1)} %wout_ref.1, bf16[512,768]{1,0:T(8,128)(2,1)} %bitcast.7), custom_call_target="tpu_custom_call" | custom-call | flops 8000000000 | bytes 6000000 | tf_op jit(solution)/shard_map/pallas_call | solution.py:368
  53.5 0.0 copy-start
  53.5 1.5 %reshape.9 = f32[9216]{0:T(1024)} reshape(f32[12,768]{1,0:T(8,128)} %get-tuple-element.7) | data formatting | bytes 73728 | tf_op jit(solution)/shard_map/reshape | solution.py:384
  55.0 2.1 %copy.12 = bf16[1,512,768]{2,1,0:T(8,128)(2,1)} copy(bf16[1,512,768]{2,1,0:T(8,128)(2,1)} %bitcast.4) | data formatting | bytes 1572864
  57.1 0.0 copy-done
  57.1 0.7 %copy.13 = f32[1,2,6,32,64]{4,3,2,1,0:T(8,128)} copy(f32[1,2,6,32,64]{4,3,2,1,0:T(8,128)S(1)} %bitcast.5) | data formatting | bytes 196608
Async XLA Ops:
  53.5 3.5 %copy-start = (f32[2,6,32,64]{3,2,1,0:T(8,128)S(1)}, f32[2,6,32,64]{3,2,1,0:T(8,128)}, u32[]{:S(2)}) copy-start(f32[2,6,32,64]{3,2,1,0:T(8,128)} %get-tuple-element.8) | copy-start | bytes 294916

commit v2 on v1

v2 whole, which is shorter than its diff:
```python
import functools
import math

import jax
import jax.numpy as jnp
from jax import lax
from jax.experimental import pallas as pl
from jax.experimental.pallas import tpu as pltpu
from jax.sharding import PartitionSpec as P

HD = 64
STRIDE = 16
FLOOR = -1e30
BF = jnp.bfloat16
F32 = jnp.float32
MESH = pl.DeviceIdType.MESH


def dot(a, b):
    return lax.dot_general(a, b, (((1,), (0,)), ((), ())), preferred_element_type=F32)


def dot_t(a, b):
    return lax.dot_general(a, b, (((1,), (1,)), ((), ())), preferred_element_type=F32)


def flip(x):
    return x.astype(F32).T.astype(BF)


def halves(x):
    high = x.astype(BF)
    return high, (x - high.astype(F32)).astype(BF)


def iota(shape, dim):
    return lax.broadcasted_iota(jnp.int32, shape, dim)


def hot(cond):
    return jnp.where(cond, 1.0, 0.0).astype(BF)


def column(row):
    return jnp.broadcast_to(row, (128, row.shape[1])).T[:, :1]


def thirds(rows):
    first = rows.astype(BF).astype(F32)
    rest = rows - first
    second = rest.astype(BF).astype(F32)
    return jnp.concatenate([first, second, rest - second, jnp.zeros_like(rows)], axis=0).astype(BF)


def joined(y):
    return y[0:8] + y[8:16] + y[16:24]


def layer(n, slides, fused, len_ref, pos_ref, tiles_hbm, wqkv_hbm, wout_hbm, cot_hbm,
          back_out, st_out, wgrad_ref, far_ref,
          tiles_ref, wqkv_ref, wout_ref, cot_ref,
          sent, psend, got, pbuf, slot_ref, st_ref, rt_ref, acc, proj, g_ref, gt_ref, kt_ref,
          vt_ref, w_ref, dp_ref, m_ref, l_ref, nt_ref, att_ref, stat_ref, kvbuf, qgbuf, stats, sbuf,
          dqt_ref, dk_ref, dv_ref, bsend, pw, wbuf, zs, zbuf,
          mask_ref, block_ref, spread_ref, back_ref, order_ref,
          in_sems, own_sems, send_sems, recv_sems, zsend, zrecv):
    me = lax.axis_index("ctx")
    my_slide = lax.axis_index("slide")
    t, d = tiles_ref.shape
    hc = wout_ref.shape[0]
    heads = hc // HD
    portion = t // n
    g = t // STRIDE
    gbits = g.bit_length() - 1
    fq = heads * g
    nf = n * g
    chunks = got.shape[0]
    wide = d // chunks

    loads = [
        pltpu.make_async_copy(src, dst, in_sems.at[i])
        for i, (src, dst) in enumerate((
            (tiles_hbm, tiles_ref), (cot_hbm, cot_ref), (wout_hbm, wout_ref), (wqkv_hbm, wqkv_ref)))
    ]
    for load in loads:
        load.start()

    barrier = pltpu.get_barrier_semaphore()

    def greet(k, carry):
        pl.semaphore_signal(barrier, inc=1, device_id={"ctx": lax.rem(me + k, n)},
                            device_id_type=MESH)
        return carry

    lax.fori_loop(1, n, greet, 0)
    if fused:
        for k in range(1, slides):
            pl.semaphore_signal(barrier, inc=1,
                                device_id={"slide": lax.rem(my_slide + k, slides)},
                                device_id_type=MESH)

    def copy_to(which, k, src, dst):
        return pltpu.make_async_remote_copy(
            src_ref=src, dst_ref=dst, send_sem=send_sems.at[which, k],
            recv_sem=recv_sems.at[which, k], device_id={"ctx": lax.rem(me + k, n)},
            device_id_type=MESH)

    def push(which, source, target):
        def body(k, carry):
            copy_to(which, k, source(lax.rem(me + k, n)), target(me)).start()
            return carry
        lax.fori_loop(1, n, body, 0)

    def landed(which, target):
        def body(k, carry):
            owner = lax.rem(me + n - k, n)
            copy_to(which, k, target(owner), target(owner)).wait_recv()
            return carry
        lax.fori_loop(1, n, body, 0)

    def left(which, target):
        def body(k, carry):
            copy_to(which, k, target(0), target(0)).wait_send()
            return carry
        lax.fori_loop(1, n, body, 0)

    length = len_ref[0]

    prow = pos_ref[...].astype(F32)
    pcol = column(prow)
    rank = jnp.sum(jnp.where(pcol < prow, 1.0, 0.0), axis=0, keepdims=True)
    down = iota((t, t), 0).astype(F32)
    across = iota((t, t), 1).astype(F32)
    pick = hot(rank == down)
    placed = column(rank) == across
    st_ref[...] = hot(placed)
    ordered = jnp.sum(jnp.where(placed, pcol, 0.0), axis=0, keepdims=True)
    psend[...] = jnp.zeros_like(psend)
    for k in range(n):
        psend[k, :, 0:portion] = jnp.broadcast_to(
            ordered[:, k * portion:(k + 1) * portion], (8, portion))
    loads[0].wait()
    for c in range(chunks):
        sent[c] = dot(pick, tiles_ref[:, c * wide:(c + 1) * wide]).astype(BF).reshape(n, portion, wide)
        if c == 0:
            pl.semaphore_wait(barrier, n - 1 + (slides - 1 if fused else 0))
            push(0, lambda peer: psend.at[peer], lambda i: pbuf.at[i])
        push(1 + c, lambda peer, c=c: sent.at[c, peer], lambda i, c=c: got.at[c, i])
    for c in range(chunks):
        got[c, me] = sent[c, me]
    pbuf[me] = psend[me]
    keep_st = pltpu.make_async_copy(st_ref, st_out, own_sems.at[0])
    keep_st.start()

    loads[1].wait()
    loads[2].wait()
    base = me * t
    live_row = base + iota((1, t), 1) < length
    live_col = base + iota((t, 1), 0) < length
    g_ref[...] = jnp.where(live_col, dot_t(cot_ref[...], wout_ref[...]), 0.0).astype(BF)
    gt_ref[...] = jnp.where(live_row, dot_t(wout_ref[...], cot_ref[...]), 0.0).astype(BF)
    gather = hot(iota((g, t), 1) >> 4 == iota((g, t), 0))
    mask_ref[...] = hot(iota((t, 1), 0) & (STRIDE - 1) == iota((1, hc), 1) >> 6)
    qgbuf[me, :, hc:2 * hc] = dot(gather, g_ref[...] * mask_ref[...]).astype(BF)
    block_ref[...] = hot(iota((fq, 1), 0) >> gbits == iota((1, hc), 1) >> 6)
    spot_col = iota((fq, 1), 0)
    spot_row = iota((1, fq), 1)
    spread_ref[...] = hot(iota((1, t), 1) == ((spot_col & (g - 1)) << 4) + (spot_col >> gbits))
    back_ref[...] = hot(iota((t, 1), 0) == ((spot_row & (g - 1)) << 4) + (spot_row >> gbits))
    m_ref[...] = jnp.zeros_like(m_ref)
    l_ref[...] = jnp.zeros_like(l_ref)
    stat_ref[...] = jnp.zeros_like(stat_ref)
    stats[...] = jnp.zeros_like(stats)
    if fused:
        run = hc // (n * slides)
        spot = iota((hc, 1), 0)
        source = (spot % (run * slides)) // run * (n * run) + spot // (run * slides) * run + spot % run
        order_ref[...] = hot(iota((1, hc), 1) == source)
        zs[...] = jnp.zeros_like(zs)
    loads[3].wait()

    landed(0, lambda i: pbuf.at[i])
    for k in range(n):
        slot_ref[:, k * portion:(k + 1) * portion] = pbuf[k, :, 0:portion]
    slot = slot_ref[0:1, :] - (me * t).astype(F32)
    rt_ref[...] = hot(column(slot) == across)
    put = hot(slot == down)
    for c in range(chunks):
        landed(1 + c, lambda i, c=c: got.at[c, i])
        sequence = dot(put, got[c].reshape(t, wide)).astype(BF)
        rows = slice(c * wide, (c + 1) * wide)
        for k in (1, 2, 0):
            cols = slice(k * hc, (k + 1) * hc)
            part = dot(sequence, wqkv_ref[rows, cols])
            if c > 0:
                part = acc[:, cols] + part
            if c < chunks - 1:
                acc[:, cols] = part
                continue
            rounded = part.astype(BF)
            proj[:, cols] = rounded
            picked = dot(gather, rounded * mask_ref[...]).astype(BF)
            if k == 0:
                qgbuf[me, :, 0:hc] = picked
                push(5, lambda peer: qgbuf.at[me], lambda i: qgbuf.at[i])
            else:
                kvbuf[me, :, (k - 1) * hc:k * hc] = picked
            if k == 2:
                push(4, lambda peer: kvbuf.at[me], lambda i: kvbuf.at[i])
    kt_ref[...] = flip(proj[:, hc:2 * hc])
    vt_ref[...] = flip(proj[:, 2 * hc:3 * hc])

    lane = iota((1, 2 * HD), 1)
    for pair in range(heads // 2):
        cols = slice(pair * 128, pair * 128 + 128)
        q2 = proj[:, cols]
        k2 = proj[:, hc + pair * 128:hc + pair * 128 + 128]
        v2 = proj[:, 2 * hc + pair * 128:2 * hc + pair * 128 + 128]
        for half in range(2):
            h = 2 * pair + half
            rows = slice(h * HD, h * HD + HD)
            mine = hot(lane >> 6 == half)
            score = jnp.where(live_col, dot_t(k2 * (mine * 0.125), q2), FLOOR)
            top = jnp.maximum(jnp.max(score, axis=0, keepdims=True), 0.5 * FLOOR)
            weight = jnp.exp(score - top)
            w_ref[h] = weight
            m_ref[h:h + 1, :] = top
            l_ref[h:h + 1, :] = jnp.sum(weight, axis=0, keepdims=True)
            nt_ref[rows, :] = dot(vt_ref[rows, :], weight.astype(BF))
            dp_ref[h] = dot(v2 * mine, gt_ref[cols, :])

    landed(4, lambda i: kvbuf.at[i])
    all_k = kvbuf[:, :, 0:hc].reshape(nf, hc)
    all_v = kvbuf[:, :, hc:2 * hc].reshape(nf, hc)
    block = block_ref[...]

    def diagonal(x):
        return jnp.concatenate([x] * heads, axis=0) * block

    own_q = diagonal(qgbuf[me, :, 0:hc])
    own_g = diagonal(qgbuf[me, :, hc:2 * hc])
    own_k = diagonal(kvbuf[me, :, 0:hc])
    own_v = diagonal(kvbuf[me, :, hc:2 * hc])
    head_rows = iota((8, fq), 0) == iota((8, fq), 1) >> gbits
    kept_cols = iota((hc, fq), 0) >> 6 == iota((hc, fq), 1) >> gbits

    def widen(row):
        return joined(dot(thirds(jnp.where(head_rows, row, 0.0)), spread_ref[...]))

    def narrow(rows):
        return jnp.sum(jnp.where(head_rows, joined(dot_t(thirds(rows), spread_ref[...])), 0.0),
                       axis=0, keepdims=True)

    def spread_cols(x):
        high, low = halves(jnp.where(kept_cols, x, 0.0))
        return dot(high, spread_ref[...]) + dot(low, spread_ref[...])

    far_live = (iota((nf, fq), 0) << 4) + (iota((nf, fq), 1) >> gbits) < length
    far_score = jnp.where(far_live, dot_t(all_k, own_q * 0.125), FLOOR)
    far_top = jnp.max(far_score, axis=0, keepdims=True)
    chosen = iota((8, t), 1) & (STRIDE - 1) == iota((8, t), 0)
    tops = m_ref[...]
    ceiling = jnp.maximum(tops, jnp.where(chosen, widen(far_top), FLOOR))
    rescale = jnp.exp(tops - ceiling)
    far_weight = jnp.where(far_live, jnp.exp(far_score - narrow(ceiling)), 0.0)
    totals = l_ref[...] * rescale + widen(jnp.sum(far_weight, axis=0, keepdims=True))
    inverse = 1.0 / jnp.where(live_row, totals, 1.0)
    inverse = jnp.where(iota((8, t), 0) < heads, inverse, 0.0)
    far_numer = spread_cols(dot(flip(all_v), far_weight.astype(BF)))
    for h in range(heads):
        rows = slice(h * HD, h * HD + HD)
        result = (nt_ref[rows, :] * rescale[h:h + 1] + far_numer[rows, :]) * inverse[h:h + 1]
        result = jnp.where(live_row, result, 0.0)
        att_ref[rows, :] = result.astype(BF)
        stat_ref[h:h + 1, :] = jnp.sum(gt_ref[rows, :].astype(F32) * result, axis=0, keepdims=True)
    stat = stat_ref[...]

    stats[0:8, :] = ceiling
    stats[8:16, :] = inverse
    stats[16:24, :] = stat
    turned = stats[...].T
    wanted = iota((t, 128), 0) & (STRIDE - 1) == iota((t, 128), 1) & 7
    sbuf[me] = jnp.sum(jnp.where(wanted, turned, 0.0).reshape(g, STRIDE, 128), axis=1)
    push(6, lambda peer: sbuf.at[me], lambda i: sbuf.at[i])

    factor = 1.0 / math.sqrt(slides * n * t)
    if fused:
        att = dot(order_ref[...], att_ref[...]).astype(BF)
        pw[...] = (dot(att, cot_ref[...]) * factor).astype(BF).reshape(n, hc // n, d)
        wbuf[me] = pw[me]
        push(7, lambda peer: pw.at[peer], lambda i: wbuf.at[i])
    else:
        wgrad_ref[...] = dot(att_ref[...], cot_ref[...]) * factor

    for pair in range(heads // 2):
        cols = slice(pair * 128, pair * 128 + 128)
        q2 = proj[:, cols] * 0.125
        g2 = g_ref[:, cols]
        key_parts = []
        value_parts = []
        for half in range(2):
            h = 2 * pair + half
            rows = slice(h * HD, h * HD + HD)
            prob = w_ref[h] * (rescale[h:h + 1] * inverse[h:h + 1])
            dscore = (prob * (dp_ref[h] - stat[h:h + 1])).astype(BF)
            dqt_ref[rows, :] = dot(kt_ref[rows, :] * 0.125, dscore)
            key_parts.append(dot(dscore, q2))
            value_parts.append(dot(prob.astype(BF), g2))
        dk_ref[:, cols] = jnp.where(lane < HD, key_parts[0], key_parts[1])
        dv_ref[:, cols] = jnp.where(lane < HD, value_parts[0], value_parts[1])

    far_prob = far_weight * narrow(inverse)
    far_dscore = far_prob * (dot_t(all_v, own_g) - narrow(stat)) * 0.125
    dqt = dqt_ref[...] + spread_cols(dot(flip(all_k), far_dscore.astype(BF)))
    proj[:, 0:hc] = dqt.T.astype(BF)
    landed(5, lambda i: qgbuf.at[i])
    all_q = qgbuf[:, :, 0:hc].reshape(nf, hc)
    all_g = qgbuf[:, :, hc:2 * hc].reshape(nf, hc)
    key_live = ((me * g + (spot_col & (g - 1))) << 4) + (spot_col >> gbits) < length
    own_score = dot_t(own_k * 0.125, all_q)
    own_dprob = dot_t(own_v, all_g)
    landed(6, lambda i: sbuf.at[i])
    rows_all = sbuf[...].reshape(nf, 128).T

    def per_head(first):
        return jnp.concatenate(
            [jnp.broadcast_to(rows_all[first + h:first + h + 1], (g, nf)) for h in range(heads)], axis=0)

    own_weight = jnp.where(key_live, jnp.exp(jnp.where(key_live, own_score - per_head(0), 0.0)), 0.0)
    own_prob = own_weight * per_head(8)
    own_dscore = own_prob * (own_dprob - per_head(16)) * 0.125
    terms = (dot(own_dscore.astype(BF), all_q), dot(own_prob.astype(BF), all_g))
    for which, base_ref in ((0, dk_ref), (1, dv_ref)):
        high, low = halves(terms[which] * block.astype(F32))
        total = base_ref[...] + dot(back_ref[...], high) + dot(back_ref[...], low)
        proj[:, (which + 1) * hc:(which + 2) * hc] = total.astype(BF)

    for c in range(chunks):
        cols = slice(c * wide, (c + 1) * wide)
        grad_seq = dot_t(proj[...], wqkv_ref[cols, :]).astype(BF)
        bsend[c] = dot(rt_ref[...], grad_seq).astype(BF).reshape(n, portion, wide)
        push(8 + c, lambda peer, c=c: bsend.at[c, peer], lambda i, cols=cols: back_out.at[i, :, cols])
    kept = [
        pltpu.make_async_copy(bsend.at[c, me], back_out.at[me, :, c * wide:(c + 1) * wide],
                              own_sems.at[1 + c]) for c in range(chunks)
    ]
    for copy in kept:
        copy.start()

    scale = math.sqrt(nf)
    for which in range(2):
        for h in range(heads):
            far_ref[which, h] = terms[which][h * g:(h + 1) * g, h * HD:(h + 1) * HD] * scale

    if fused:
        def slide_copy(k, src, dst):
            return pltpu.make_async_remote_copy(
                src_ref=src, dst_ref=dst, send_sem=zsend.at[k], recv_sem=zrecv.at[k],
                device_id={"slide": lax.rem(my_slide + k, slides)}, device_id_type=MESH)

        landed(7, lambda i: wbuf.at[i])
        summed = jnp.sum(wbuf[...].astype(F32), axis=0)
        for k in range(slides):
            zs[k, 0:run, :] = summed[k * run:(k + 1) * run, :]
        for k in range(1, slides):
            slide_copy(k, zs.at[lax.rem(my_slide + k, slides)], zbuf.at[my_slide]).start()
        zbuf[my_slide] = zs[my_slide]
        for k in range(1, slides):
            owner = lax.rem(my_slide + slides - k, slides)
            slide_copy(k, zbuf.at[owner], zbuf.at[owner]).wait_recv()
        share = jnp.sum(zbuf[...], axis=0)[0:run, :]
        for j in range(d // 128):
            wgrad_ref[pl.ds(j, run, stride=d // 128), :] = share[:, j * 128:(j + 1) * 128]
        for k in range(1, slides):
            slide_copy(k, zs.at[0], zbuf.at[0]).wait_send()
        left(7, lambda i: wbuf.at[i])
    left(0, lambda i: pbuf.at[i])
    for c in range(chunks):
        left(1 + c, lambda i, c=c: got.at[c, i])
    left(4, lambda i: kvbuf.at[i])
    left(5, lambda i: qgbuf.at[i])
    left(6, lambda i: sbuf.at[i])
    keep_st.wait()
    for copy in kept:
        copy.wait()
    for c in range(chunks):
        cols = slice(c * wide, (c + 1) * wide)
        landed(8 + c, lambda i, cols=cols: back_out.at[i, :, cols])
        left(8 + c, lambda i, c=c: bsend.at[c, i])


def local(slides, n, tiles, tile_pos, lengths, qkv_weight, out_weight, cotangent):
    _, t, d = tiles.shape
    hc = out_weight.shape[0]
    heads = hc // HD
    portion = t // n
    g = t // STRIDE
    fused = hc % (n * slides) == 0 and (hc // n) % 16 == 0
    run = hc // (n * slides) if fused else 0
    pad = -(-run // 8) * 8 if fused else 8
    wrows = hc // n if fused else 16
    chunks = 3
    wide = d // chunks
    fq = heads * g
    vm = pltpu.VMEM
    dma = pltpu.SemaphoreType.DMA
    scratch = [
        vm((t, d), BF), vm(qkv_weight.shape, BF), vm(out_weight.shape, BF), vm((t, d), BF),
        vm((chunks, n, portion, wide), BF), vm((n, 8, 128), F32), vm((chunks, n, portion, wide), BF),
        vm((n, 8, 128), F32), vm((8, t), F32), vm((t, t), BF), vm((t, t), BF),
        vm((t, 3 * hc), F32), vm((t, 3 * hc), BF), vm((t, hc), BF), vm((hc, t), BF),
        vm((hc, t), BF), vm((hc, t), BF),
        vm((heads, t, t), F32), vm((heads, t, t), F32), vm((8, t), F32), vm((8, t), F32),
        vm((hc, t), F32), vm((hc, t), BF), vm((8, t), F32),
        vm((n, g, 2 * hc), BF), vm((n, g, 2 * hc), BF), vm((128, t), F32), vm((n, g, 128), F32),
        vm((hc, t), F32), vm((t, hc), F32), vm((t, hc), F32),
        vm((chunks, n, portion, wide), BF),
        vm((n, wrows, d), BF), vm((n, wrows, d), BF),
        vm((slides, pad, d), F32), vm((slides, pad, d), F32),
        vm((t, hc), BF), vm((fq, hc), BF), vm((fq, t), BF), vm((t, fq), BF), vm((hc, hc), BF),
        dma((4,)), dma((1 + chunks,)), dma((8 + chunks, n)), dma((8 + chunks, n)),
        dma((slides,)), dma((slides,)),
    ]
    spec = pl.BlockSpec(memory_space=pltpu.VMEM)
    any_spec = pl.BlockSpec(memory_space=pl.ANY)
    back, placing, wgrad, far = pl.pallas_call(
        functools.partial(layer, n, slides, fused),
        out_shape=(
            jax.ShapeDtypeStruct((n, portion, d), BF),
            jax.ShapeDtypeStruct((t, t), BF),
            jax.ShapeDtypeStruct((run * d // 128, 128) if fused else (hc, d), F32),
            jax.ShapeDtypeStruct((2, heads, g, HD), F32),
        ),
        in_specs=[pl.BlockSpec(memory_space=pltpu.SMEM), spec] + [any_spec] * 4,
        out_specs=(any_spec, any_spec, spec, spec),
        scratch_shapes=scratch,
        compiler_params=pltpu.CompilerParams(
            collective_id=0, has_side_effects=True, vmem_limit_bytes=56 * 1024 * 1024
        ),
        cost_estimate=pl.CostEstimate(flops=8 * 10**9, bytes_accessed=6 * 10**6, transcendentals=2 * 10**6),
    )(lengths, tile_pos, tiles[0], qkv_weight, out_weight, cotangent[0])
    grads = dot(placing, back.reshape(t, d)).astype(BF)
    if fused:
        wgrad = wgrad.reshape(-1)
    else:
        wgrad = lax.psum_scatter(
            wgrad.reshape(-1), ("slide", "ctx"), scatter_dimension=0, tiled=True
        )
    return grads[None], wgrad, far[None]


def solution(mesh):
    placed = (
        P("slide", "ctx", None),
        P("slide", "ctx"),
        P("slide"),
        P(),
        P(),
        P("slide", "ctx", None),
    )
    return jax.shard_map(
        functools.partial(local, mesh.shape["slide"], mesh.shape["ctx"]),
        mesh=mesh,
        in_specs=placed,
        out_specs=(
            P("slide", "ctx", None),
            P(("slide", "ctx")),
            P("slide", None, None, "ctx", None),
        ),
        check_vma=False,
    )
```

time: 57.9 us -> 51.9 us (0.90)
  Pallas kernels: 52.2 us -> 46.3 us
  local copies, waits for them, and re-layouts: 4.2 us -> 1.3 us
  matrix products: 0 us -> 2.78 us
    pallas_call x1, Pallas kernels: 52.2 us -> 46.3 us  [local(): pl.pallas_call(functools.partial(layer, n, slides, fused), out_shape=(jax...]
    dot_general x0 -> x1, matrix products: none -> 2.78 us  [dot(): lax.dot_general(a, b, (((1,), (0,)), ((), ())), preferred_element_type=F32)]
    reshape x1 -> x0, local copies, waits for them, and re-layouts: 1.46 us -> none  [local(): wgrad = wgrad.reshape(-1)]
    unnamed x4 -> x6, local copies, waits for them, and re-layouts: 2.74 us -> 1.3 us
where the time goes in v2:
time: 51.9 us; the launch traced here: 51.7 us
  Pallas kernels  46.3 us (89%)
  matrix products  2.78 us (5%)
  local copies, waits for them, and re-layouts  1.3 us (3%)
  between operations  1.3 us (3%)
    pallas_call x1, Pallas kernels, local(): pl.pallas_call(functools.partial(layer, n, slides, fused), out_shape=(jax...  46.3 us
    dot_general x1, matrix products, dot(): lax.dot_general(a, b, (((1,), (0,)), ((), ())), preferred_element_type=F32)  2.78 us
    unnamed x6, local copies, waits for them, and re-layouts  1.3 us

profile of v2, /device:TPU:1, one launch (start us, length us, event | category | flops | bytes accessed | tf_op | source)
XLA Modules:
  0.0 51.7 jit_solution(8322814143406146481)
XLA Ops:
  1.3 46.3 %shard_map.85 = (bf16[8,64,768]{2,1,0:T(8,128)(2,1)}, bf16[512,512]{1,0:T(8,128)(2,1)}, f32[72,128]{1,0:T(8,128)}, f32[2,6,32,64]{3,2,1,0:T(8,128)}) custom-call(s32[1]{0:T(128)S(6)} %copy.11.len_ref, s32[1,512]{1,0:T(1,128)} %pos_ref.1, bf16[512,768]{1,0:T(8,128)(2,1)} %bitcast.11, bf16[768,1152]{1,0:T(8,128)(2,1)} %wqkv_hbm.1, bf16[384,768]{1,0:T(8,128)(2,1)} %wout_hbm.1, ...), custom_call_target="tpu_custom_call" | custom-call | flops 8000000000 | bytes 6000000 | tf_op jit(solution)/shard_map/pallas_call | solution.py:426
  47.6 0.0 copy-start.1
  47.6 0.0 copy-start
  47.6 2.8 %fusion = bf16[1,512,768]{2,1,0:T(8,128)(2,1)} fusion(bf16[512,512]{1,0:T(8,128)(2,1)} %get-tuple-element.7, bf16[512,768]{1,0:T(8,128)(2,1)} %bitcast.13), kind=kOutput, calls=%fused_computation.1 | convolution fusion | flops 403046400 | bytes 2097152 | tf_op jit(solution)/shard_map/dot_general | solution.py:20
  50.4 0.0 copy-done.1
  50.4 0.6 %copy.12 = f32[9216]{0:T(1024)} copy(f32[9216]{0:T(1024)S(1)} %bitcast.10) | data formatting | bytes 73728
  51.0 0.0 copy-done
  51.0 0.7 %copy.13 = f32[1,2,6,32,64]{4,3,2,1,0:T(8,128)} copy(f32[1,2,6,32,64]{4,3,2,1,0:T(8,128)S(1)} %bitcast.9) | data formatting | bytes 196608
Async XLA Ops:
  47.6 2.8 %copy-start.1 = (f32[72,128]{1,0:T(8,128)S(1)}, f32[72,128]{1,0:T(8,128)}, u32[]{:S(2)}) copy-start(f32[72,128]{1,0:T(8,128)} %get-tuple-element.9) | copy-start | bytes 110596
  47.6 3.4 %copy-start = (f32[2,6,32,64]{3,2,1,0:T(8,128)S(1)}, f32[2,6,32,64]{3,2,1,0:T(8,128)}, u32[]{:S(2)}) copy-start(f32[2,6,32,64]{3,2,1,0:T(8,128)} %get-tuple-element.10) | copy-start | bytes 294916

commit v3 on v2

--- a/solution.py
+++ b/solution.py
@@ -62,7 +62,7 @@
           sent, psend, got, pbuf, slot_ref, st_ref, rt_ref, acc, proj, g_ref, gt_ref, kt_ref,
           vt_ref, w_ref, dp_ref, m_ref, l_ref, nt_ref, att_ref, stat_ref, kvbuf, qgbuf, stats, sbuf,
           dqt_ref, dk_ref, dv_ref, bsend, pw, wbuf, zs, zbuf,
-          mask_ref, block_ref, spread_ref, back_ref, order_ref,
+          block_ref, spread_ref, order_ref,
           in_sems, own_sems, send_sems, recv_sems, zsend, zrecv):
     me = lax.axis_index("ctx")
     my_slide = lax.axis_index("slide")
@@ -157,16 +157,40 @@
     base = me * t
     live_row = base + iota((1, t), 1) < length
     live_col = base + iota((t, 1), 0) < length
-    g_ref[...] = jnp.where(live_col, dot_t(cot_ref[...], wout_ref[...]), 0.0).astype(BF)
     gt_ref[...] = jnp.where(live_row, dot_t(wout_ref[...], cot_ref[...]), 0.0).astype(BF)
-    gather = hot(iota((g, t), 1) >> 4 == iota((g, t), 0))
-    mask_ref[...] = hot(iota((t, 1), 0) & (STRIDE - 1) == iota((1, hc), 1) >> 6)
-    qgbuf[me, :, hc:2 * hc] = dot(gather, g_ref[...] * mask_ref[...]).astype(BF)
+    lane = iota((1, 2 * HD), 1)
+
+    pairs = heads // 2
+
+    def fill(ref, start, value):
+        for pair in range(pairs):
+            ref[start + pair] = value[:, pair * 128:pair * 128 + 128]
+
+    def taken(ref, start):
+        return jnp.concatenate([ref[start + pair] for pair in range(pairs)], axis=1)
+
+    def far_rows(start):
+        parts = []
+        for pair in range(pairs):
+            parts.append(jnp.where(
+                lane < HD,
+                acc[start + pair, pl.ds(2 * pair, g, stride=STRIDE), :],
+                acc[start + pair, pl.ds(2 * pair + 1, g, stride=STRIDE), :]))
+        return jnp.concatenate(parts, axis=1).astype(BF)
+
+    def add_far_rows(ref, term):
+        for h in range(heads):
+            cols = slice(h // 2 * 128, h // 2 * 128 + 128)
+            spot = (h // 2, pl.ds(h, g, stride=STRIDE), slice(None))
+            ref[spot] = ref[spot] + jnp.where(lane >> 6 == h % 2, term[h * g:(h + 1) * g, cols], 0.0)
+
+    grad_rows = jnp.where(live_col, dot_t(cot_ref[...], wout_ref[...]), 0.0)
+    fill(acc, 0, grad_rows)
+    g_ref[...] = grad_rows.astype(BF)
+    qgbuf[me, :, hc:2 * hc] = far_rows(0)
     block_ref[...] = hot(iota((fq, 1), 0) >> gbits == iota((1, hc), 1) >> 6)
     spot_col = iota((fq, 1), 0)
-    spot_row = iota((1, fq), 1)
     spread_ref[...] = hot(iota((1, t), 1) == ((spot_col & (g - 1)) << 4) + (spot_col >> gbits))
-    back_ref[...] = hot(iota((t, 1), 0) == ((spot_row & (g - 1)) << 4) + (spot_row >> gbits))
     m_ref[...] = jnp.zeros_like(m_ref)
     l_ref[...] = jnp.zeros_like(l_ref)
     stat_ref[...] = jnp.zeros_like(stat_ref)
@@ -193,13 +217,12 @@
             cols = slice(k * hc, (k + 1) * hc)
             part = dot(sequence, wqkv_ref[rows, cols])
             if c > 0:
-                part = acc[:, cols] + part
+                part = taken(acc, k * pairs) + part
+            fill(acc, k * pairs, part)
             if c < chunks - 1:
-                acc[:, cols] = part
                 continue
-            rounded = part.astype(BF)
-            proj[:, cols] = rounded
-            picked = dot(gather, rounded * mask_ref[...]).astype(BF)
+            proj[:, cols] = part.astype(BF)
+            picked = far_rows(k * pairs)
             if k == 0:
                 qgbuf[me, :, 0:hc] = picked
                 push(5, lambda peer: qgbuf.at[me], lambda i: qgbuf.at[i])
@@ -210,7 +233,6 @@
     kt_ref[...] = flip(proj[:, hc:2 * hc])
     vt_ref[...] = flip(proj[:, 2 * hc:3 * hc])
 
-    lane = iota((1, 2 * HD), 1)
     for pair in range(heads // 2):
         cols = slice(pair * 128, pair * 128 + 128)
         q2 = proj[:, cols]
@@ -244,12 +266,15 @@
     head_rows = iota((8, fq), 0) == iota((8, fq), 1) >> gbits
     kept_cols = iota((hc, fq), 0) >> 6 == iota((hc, fq), 1) >> gbits
 
-    def widen(row):
-        return joined(dot(thirds(jnp.where(head_rows, row, 0.0)), spread_ref[...]))
-
-    def narrow(rows):
-        return jnp.sum(jnp.where(head_rows, joined(dot_t(thirds(rows), spread_ref[...])), 0.0),
-                       axis=0, keepdims=True)
+    def widen(first, second):
+        rows = [thirds(jnp.where(head_rows, row, 0.0)) for row in (first, second)]
+        y = dot(jnp.concatenate(rows, axis=0), spread_ref[...])
+        return joined(y[0:32]), joined(y[32:64])
+
+    def narrow(first, second):
+        y = dot_t(jnp.concatenate([thirds(first), thirds(second)], axis=0), spread_ref[...])
+        return [jnp.sum(jnp.where(head_rows, joined(y[k:k + 32]), 0.0), axis=0, keepdims=True)
+                for k in (0, 32)]
 
     def spread_cols(x):
         high, low = halves(jnp.where(kept_cols, x, 0.0))
@@ -257,19 +282,24 @@
 
     far_live = (iota((nf, fq), 0) << 4) + (iota((nf, fq), 1) >> gbits) < length
     far_score = jnp.where(far_live, dot_t(all_k, own_q * 0.125), FLOOR)
-    far_top = jnp.max(far_score, axis=0, keepdims=True)
+    far_top = jnp.maximum(jnp.max(far_score, axis=0, keepdims=True), 0.5 * FLOOR)
+    far_weight = jnp.exp(far_score - far_top)
+    far_tops, far_sums = widen(far_top, jnp.sum(far_weight, axis=0, keepdims=True))
+    far_numer = spread_cols(dot(flip(all_v), far_weight.astype(BF)))
     chosen = iota((8, t), 1) & (STRIDE - 1) == iota((8, t), 0)
     tops = m_ref[...]
-    ceiling = jnp.maximum(tops, jnp.where(chosen, widen(far_top), FLOOR))
+    far_tops = jnp.where(chosen, far_tops, FLOOR)
+    ceiling = jnp.maximum(tops, far_tops)
     rescale = jnp.exp(tops - ceiling)
-    far_weight = jnp.where(far_live, jnp.exp(far_score - narrow(ceiling)), 0.0)
-    totals = l_ref[...] * rescale + widen(jnp.sum(far_weight, axis=0, keepdims=True))
+    far_rescale = jnp.exp(far_tops - ceiling)
+    totals = l_ref[...] * rescale + far_sums * far_rescale
     inverse = 1.0 / jnp.where(live_row, totals, 1.0)
     inverse = jnp.where(iota((8, t), 0) < heads, inverse, 0.0)
-    far_numer = spread_cols(dot(flip(all_v), far_weight.astype(BF)))
+    near_part = rescale * inverse
+    far_part = far_rescale * inverse
     for h in range(heads):
         rows = slice(h * HD, h * HD + HD)
-        result = (nt_ref[rows, :] * rescale[h:h + 1] + far_numer[rows, :]) * inverse[h:h + 1]
+        result = nt_ref[rows, :] * near_part[h:h + 1] + far_numer[rows, :] * far_part[h:h + 1]
         result = jnp.where(live_row, result, 0.0)
         att_ref[rows, :] = result.astype(BF)
         stat_ref[h:h + 1, :] = jnp.sum(gt_ref[rows, :].astype(F32) * result, axis=0, keepdims=True)
@@ -301,18 +331,20 @@
         for half in range(2):
             h = 2 * pair + half
             rows = slice(h * HD, h * HD + HD)
-            prob = w_ref[h] * (rescale[h:h + 1] * inverse[h:h + 1])
+            prob = w_ref[h] * near_part[h:h + 1]
             dscore = (prob * (dp_ref[h] - stat[h:h + 1])).astype(BF)
             dqt_ref[rows, :] = dot(kt_ref[rows, :] * 0.125, dscore)
             key_parts.append(dot(dscore, q2))
             value_parts.append(dot(prob.astype(BF), g2))
-        dk_ref[:, cols] = jnp.where(lane < HD, key_parts[0], key_parts[1])
-        dv_ref[:, cols] = jnp.where(lane < HD, value_parts[0], value_parts[1])
-
-    far_prob = far_weight * narrow(inverse)
-    far_dscore = far_prob * (dot_t(all_v, own_g) - narrow(stat)) * 0.125
-    dqt = dqt_ref[...] + spread_cols(dot(flip(all_k), far_dscore.astype(BF)))
-    proj[:, 0:hc] = dqt.T.astype(BF)
+        dk_ref[pair] = jnp.where(lane < HD, key_parts[0], key_parts[1])
+        dv_ref[pair] = jnp.where(lane < HD, value_parts[0], value_parts[1])
+
+    far_unit, far_stat = narrow(far_part, stat)
+    far_dscore = far_weight * far_unit * (dot_t(all_v, own_g) - far_stat)
+    far_dq = dot(flip(all_k * 0.125), far_dscore.astype(BF))
+    fill(acc, 0, dqt_ref[...].T)
+    add_far_rows(acc, far_dq.T)
+    proj[:, 0:hc] = taken(acc, 0).astype(BF)
     landed(5, lambda i: qgbuf.at[i])
     all_q = qgbuf[:, :, 0:hc].reshape(nf, hc)
     all_g = qgbuf[:, :, hc:2 * hc].reshape(nf, hc)
@@ -331,9 +363,8 @@
     own_dscore = own_prob * (own_dprob - per_head(16)) * 0.125
     terms = (dot(own_dscore.astype(BF), all_q), dot(own_prob.astype(BF), all_g))
     for which, base_ref in ((0, dk_ref), (1, dv_ref)):
-        high, low = halves(terms[which] * block.astype(F32))
-        total = base_ref[...] + dot(back_ref[...], high) + dot(back_ref[...], low)
-        proj[:, (which + 1) * hc:(which + 2) * hc] = total.astype(BF)
+        add_far_rows(base_ref, terms[which])
+        proj[:, (which + 1) * hc:(which + 2) * hc] = taken(base_ref, 0).astype(BF)
 
     for c in range(chunks):
         cols = slice(c * wide, (c + 1) * wide)
@@ -347,10 +378,9 @@
     for copy in kept:
         copy.start()
 
-    scale = math.sqrt(nf)
     for which in range(2):
         for h in range(heads):
-            far_ref[which, h] = terms[which][h * g:(h + 1) * g, h * HD:(h + 1) * HD] * scale
+            far_ref[which, h] = terms[which][h * g:(h + 1) * g, h * HD:(h + 1) * HD]
 
     if fused:
         def slide_copy(k, src, dst):
@@ -389,6 +419,18 @@
         left(8 + c, lambda i, c=c: bsend.at[c, i])
 
 
+def finish(placing_ref, back_ref, far_in, *rest):
+    wgrad_in = rest[:(len(rest) - 2) // 2]
+    grads_ref, far_ref = rest[len(wgrad_in):len(wgrad_in) + 2]
+    grads_ref[...] = dot(placing_ref[...], back_ref[...]).astype(BF)
+
+    @pl.when(pl.program_id(0) == 0)
+    def small():
+        far_ref[...] = far_in[...] * math.sqrt(far_in.shape[2] * lax.axis_size("ctx"))
+        for source, target in zip(wgrad_in, rest[len(wgrad_in) + 2:]):
+            target[...] = source[...]
+
+
 def local(slides, n, tiles, tile_pos, lengths, qkv_weight, out_weight, cotangent):
     _, t, d = tiles.shape
     hc = out_weight.shape[0]
@@ -408,16 +450,16 @@
         vm((t, d), BF), vm(qkv_weight.shape, BF), vm(out_weight.shape, BF), vm((t, d), BF),
         vm((chunks, n, portion, wide), BF), vm((n, 8, 128), F32), vm((chunks, n, portion, wide), BF),
         vm((n, 8, 128), F32), vm((8, t), F32), vm((t, t), BF), vm((t, t), BF),
-        vm((t, 3 * hc), F32), vm((t, 3 * hc), BF), vm((t, hc), BF), vm((hc, t), BF),
+        vm((3 * hc // 128, t, 128), F32), vm((t, 3 * hc), BF), vm((t, hc), BF), vm((hc, t), BF),
         vm((hc, t), BF), vm((hc, t), BF),
         vm((heads, t, t), F32), vm((heads, t, t), F32), vm((8, t), F32), vm((8, t), F32),
         vm((hc, t), F32), vm((hc, t), BF), vm((8, t), F32),
         vm((n, g, 2 * hc), BF), vm((n, g, 2 * hc), BF), vm((128, t), F32), vm((n, g, 128), F32),
-        vm((hc, t), F32), vm((t, hc), F32), vm((t, hc), F32),
+        vm((hc, t), F32), vm((heads // 2, t, 128), F32), vm((heads // 2, t, 128), F32),
         vm((chunks, n, portion, wide), BF),
         vm((n, wrows, d), BF), vm((n, wrows, d), BF),
         vm((slides, pad, d), F32), vm((slides, pad, d), F32),
-        vm((t, hc), BF), vm((fq, hc), BF), vm((fq, t), BF), vm((t, fq), BF), vm((hc, hc), BF),
+        vm((fq, hc), BF), vm((fq, t), BF), vm((hc, hc), BF),
         dma((4,)), dma((1 + chunks,)), dma((8 + chunks, n)), dma((8 + chunks, n)),
         dma((slides,)), dma((slides,)),
     ]
@@ -439,9 +481,26 @@
         ),
         cost_estimate=pl.CostEstimate(flops=8 * 10**9, bytes_accessed=6 * 10**6, transcendentals=2 * 10**6),
     )(lengths, tile_pos, tiles[0], qkv_weight, out_weight, cotangent[0])
-    grads = dot(placing, back.reshape(t, d)).astype(BF)
+    grads, far, *rest = pl.pallas_call(
+        finish,
+        grid=(chunks,),
+        out_shape=(
+            jax.ShapeDtypeStruct((t, d), BF),
+            jax.ShapeDtypeStruct(far.shape, F32),
+        ) + ((jax.ShapeDtypeStruct(wgrad.shape, F32),) if fused else ()),
+        in_specs=[
+            pl.BlockSpec((t, t), lambda i: (0, 0)),
+            pl.BlockSpec((t, wide), lambda i: (0, i)),
+            pl.BlockSpec(far.shape, lambda i: (0, 0, 0, 0)),
+        ] + [pl.BlockSpec(wgrad.shape, lambda i: (0, 0))] * fused,
+        out_specs=(
+            pl.BlockSpec((t, wide), lambda i: (0, i)),
+            pl.BlockSpec(far.shape, lambda i: (0, 0, 0, 0)),
+        ) + (pl.BlockSpec(wgrad.shape, lambda i: (0, 0)),) * fused,
+        cost_estimate=pl.CostEstimate(flops=2 * t * t * d, bytes_accessed=3 * 10**6, transcendentals=0),
+    )(placing, back.reshape(t, d), far, *([wgrad] * fused))
     if fused:
-        wgrad = wgrad.reshape(-1)
+        wgrad = rest[0].reshape(-1)
     else:
         wgrad = lax.psum_scatter(
             wgrad.reshape(-1), ("slide", "ctx"), scatter_dimension=0, tiled=True

time: 51.9 us -> 51.3 us (0.988)
  Pallas kernels: 46.3 us -> 49.5 us
  matrix products: 2.78 us -> 0 us
  local copies, waits for them, and re-layouts: 1.3 us -> 0 us
    pallas_call x0 -> x1, Pallas kernels: none -> 3.63 us  [local(): pl.pallas_call(finish, grid=(chunks,), out_shape=(jax.ShapeDtypeStruct((t...]
    dot_general x1 -> x0, matrix products: 2.78 us -> none  [dot(): lax.dot_general(a, b, (((1,), (0,)), ((), ())), preferred_element_type=F32)]
    unnamed x6 -> x0, local copies, waits for them, and re-layouts: 1.3 us -> none
where the time goes in v3:
time: 51.3 us; the launch traced here: 50.8 us
  Pallas kernels  49.5 us (96%)
  between operations  1.29 us (3%)
    pallas_call x1, Pallas kernels, local(): pl.pallas_call(functools.partial(layer, n, slides, fused), out_shape=(jax...  45.9 us
    pallas_call x1, Pallas kernels, local(): pl.pallas_call(finish, grid=(chunks,), out_shape=(jax.ShapeDtypeStruct((t...  3.63 us

profile of v3, /device:TPU:1, one launch (start us, length us, event | category | flops | bytes accessed | tf_op | source)
XLA Modules:
  0.0 50.8 jit_solution(4083145108749573364)
XLA Ops:
  1.3 45.9 %shard_map.85 = (bf16[8,64,768]{2,1,0:T(8,128)(2,1)}, bf16[512,512]{1,0:T(8,128)(2,1)}, f32[72,128]{1,0:T(8,128)}, f32[2,6,32,64]{3,2,1,0:T(8,128)}) custom-call(s32[1]{0:T(128)S(6)} %copy.9.len_ref, s32[1,512]{1,0:T(1,128)} %pos_ref.1, bf16[512,768]{1,0:T(8,128)(2,1)} %bitcast.7, bf16[768,1152]{1,0:T(8,128)(2,1)} %wqkv_hbm.1, bf16[384,768]{1,0:T(8,128)(2,1)} %wout_hbm.1, ...), custom_call_target="tpu_custom_call" | custom-call | flops 8000000000 | bytes 6000000 | tf_op jit(solution)/shard_map/pallas_call | solution.py:468
  47.2 3.6 %shard_map.86 = (bf16[512,768]{1,0:T(8,128)(2,1)}, f32[2,6,32,64]{3,2,1,0:T(8,128)}, f32[72,128]{1,0:T(8,128)}) custom-call(bf16[512,512]{1,0:T(8,128)(2,1)} %get-tuple-element.10.placing_ref, bf16[512,768]{1,0:T(8,128)(2,1)} %bitcast.6, f32[2,6,32,64]{3,2,1,0:T(8,128)} %get-tuple-element.12.far_in, f32[72,128]{1,0:T(8,128)} %get-tuple-element.13.rest_0_), custom_call_target="tpu_custom_call" | custom-call | flops 402653184 | bytes 3000000 | tf_op jit(solution)/shard_map/pallas_call | solution.py:484

commit v4 on v3

--- a/solution.py
+++ b/solution.py
@@ -61,7 +61,7 @@
           tiles_ref, wqkv_ref, wout_ref, cot_ref,
           sent, psend, got, pbuf, slot_ref, st_ref, rt_ref, acc, proj, g_ref, gt_ref, kt_ref,
           vt_ref, w_ref, dp_ref, m_ref, l_ref, nt_ref, att_ref, stat_ref, kvbuf, qgbuf, stats, sbuf,
-          dqt_ref, dk_ref, dv_ref, bsend, pw, wbuf, zs, zbuf,
+          dqt_ref, dk_ref, dv_ref, bsend, pw, wbuf, zs, zbuf, cs, cbuf,
           block_ref, spread_ref, order_ref,
           in_sems, own_sems, send_sems, recv_sems, zsend, zrecv):
     me = lax.axis_index("ctx")
@@ -124,6 +124,46 @@
             return carry
         lax.fori_loop(1, n, body, 0)
 
+    chips = n // 2
+    core = lax.rem(me, 2)
+    chip = lax.div(me, 2)
+    partner = 2 * chip + 1 - core
+
+    def hop(which, k, peer, src, dst):
+        return pltpu.make_async_remote_copy(
+            src_ref=src, dst_ref=dst, send_sem=send_sems.at[which, k],
+            recv_sem=recv_sems.at[which, k], device_id={"ctx": peer}, device_id_type=MESH)
+
+    def across_chips(k):
+        return 2 * lax.rem(chip + k, chips) + core
+
+    def behind(k, side):
+        return 2 * lax.rem(chip + chips - k, chips) + side
+
+    def spread_own(which, buf):
+        def body(k, carry):
+            hop(which, k, across_chips(k), buf.at[me], buf.at[me]).start()
+            return carry
+        lax.fori_loop(1, chips, body, 0)
+        hop(which, chips, partner, buf.at[me], buf.at[me]).start()
+
+    def hand_on(which, buf):
+        def body(k, carry):
+            block = buf.at[behind(k, core)]
+            hop(which, k, partner, block, block).wait_recv()
+            hop(which, chips + k, partner, block, block).start()
+            return carry
+        lax.fori_loop(1, chips, body, 0)
+
+    def gathered(which, buf):
+        hop(which, chips, partner, buf.at[partner], buf.at[partner]).wait_recv()
+
+        def body(k, carry):
+            block = buf.at[behind(k, 1 - core)]
+            hop(which, chips + k, partner, block, block).wait_recv()
+            return carry
+        lax.fori_loop(1, chips, body, 0)
+
     length = len_ref[0]
 
     prow = pos_ref[...].astype(F32)
@@ -198,9 +238,11 @@
     if fused:
         run = hc // (n * slides)
         spot = iota((hc, 1), 0)
-        source = (spot % (run * slides)) // run * (n * run) + spot // (run * slides) * run + spot % run
+        side, spot = spot // (hc // 2), spot % (hc // 2)
+        slab, spot = spot // (run * chips), spot % (run * chips)
+        source = (slab * n + 2 * (spot // run) + side) * run + spot % run
         order_ref[...] = hot(iota((1, hc), 1) == source)
-        zs[...] = jnp.zeros_like(zs)
+        cs[...] = jnp.zeros_like(cs)
     loads[3].wait()
 
     landed(0, lambda i: pbuf.at[i])
@@ -225,11 +267,11 @@
             picked = far_rows(k * pairs)
             if k == 0:
                 qgbuf[me, :, 0:hc] = picked
-                push(5, lambda peer: qgbuf.at[me], lambda i: qgbuf.at[i])
+                spread_own(5, qgbuf)
             else:
                 kvbuf[me, :, (k - 1) * hc:k * hc] = picked
             if k == 2:
-                push(4, lambda peer: kvbuf.at[me], lambda i: kvbuf.at[i])
+                spread_own(4, kvbuf)
     kt_ref[...] = flip(proj[:, hc:2 * hc])
     vt_ref[...] = flip(proj[:, 2 * hc:3 * hc])
 
@@ -250,8 +292,10 @@
             l_ref[h:h + 1, :] = jnp.sum(weight, axis=0, keepdims=True)
             nt_ref[rows, :] = dot(vt_ref[rows, :], weight.astype(BF))
             dp_ref[h] = dot(v2 * mine, gt_ref[cols, :])
-
-    landed(4, lambda i: kvbuf.at[i])
+        if pair == heads // 2 - 2:
+            hand_on(4, kvbuf)
+
+    gathered(4, kvbuf)
     all_k = kvbuf[:, :, 0:hc].reshape(nf, hc)
     all_v = kvbuf[:, :, hc:2 * hc].reshape(nf, hc)
     block = block_ref[...]
@@ -316,11 +360,18 @@
     factor = 1.0 / math.sqrt(slides * n * t)
     if fused:
         att = dot(order_ref[...], att_ref[...]).astype(BF)
-        pw[...] = (dot(att, cot_ref[...]) * factor).astype(BF).reshape(n, hc // n, d)
-        wbuf[me] = pw[me]
-        push(7, lambda peer: pw.at[peer], lambda i: wbuf.at[i])
+        pw[...] = (dot(att, cot_ref[...]) * factor).reshape(2, hc // 2, d)
+        pair_copy = hop(7, chips, partner, pw.at[1 - core], wbuf)
+        pair_copy.start()
     else:
         wgrad_ref[...] = dot(att_ref[...], cot_ref[...]) * factor
+
+    hand_on(5, qgbuf)
+
+    def slide_copy(k, src, dst):
+        return pltpu.make_async_remote_copy(
+            src_ref=src, dst_ref=dst, send_sem=zsend.at[k], recv_sem=zrecv.at[k],
+            device_id={"slide": lax.rem(my_slide + k, slides)}, device_id_type=MESH)
 
     for pair in range(heads // 2):
         cols = slice(pair * 128, pair * 128 + 128)
@@ -338,6 +389,12 @@
             value_parts.append(dot(prob.astype(BF), g2))
         dk_ref[pair] = jnp.where(lane < HD, key_parts[0], key_parts[1])
         dv_ref[pair] = jnp.where(lane < HD, value_parts[0], value_parts[1])
+        if fused and pair == 0:
+            pair_copy.wait_recv()
+            zs[...] = (pw[core] + wbuf[...]).astype(BF).reshape(zs.shape)
+            for k in range(1, slides):
+                slide_copy(k, zs.at[lax.rem(my_slide + k, slides)], zbuf.at[my_slide]).start()
+            zbuf[my_slide] = zs[my_slide]
 
     far_unit, far_stat = narrow(far_part, stat)
     far_dscore = far_weight * far_unit * (dot_t(all_v, own_g) - far_stat)
@@ -345,7 +402,7 @@
     fill(acc, 0, dqt_ref[...].T)
     add_far_rows(acc, far_dq.T)
     proj[:, 0:hc] = taken(acc, 0).astype(BF)
-    landed(5, lambda i: qgbuf.at[i])
+    gathered(5, qgbuf)
     all_q = qgbuf[:, :, 0:hc].reshape(nf, hc)
     all_g = qgbuf[:, :, hc:2 * hc].reshape(nf, hc)
     key_live = ((me * g + (spot_col & (g - 1))) << 4) + (spot_col >> gbits) < length
@@ -380,30 +437,29 @@
 
     for which in range(2):
         for h in range(heads):
-            far_ref[which, h] = terms[which][h * g:(h + 1) * g, h * HD:(h + 1) * HD]
+            far_ref[which, h] = terms[which][h * g:(h + 1) * g, h * HD:(h + 1) * HD] * math.sqrt(nf)
 
     if fused:
-        def slide_copy(k, src, dst):
-            return pltpu.make_async_remote_copy(
-                src_ref=src, dst_ref=dst, send_sem=zsend.at[k], recv_sem=zrecv.at[k],
-                device_id={"slide": lax.rem(my_slide + k, slides)}, device_id_type=MESH)
-
-        landed(7, lambda i: wbuf.at[i])
-        summed = jnp.sum(wbuf[...].astype(F32), axis=0)
-        for k in range(slides):
-            zs[k, 0:run, :] = summed[k * run:(k + 1) * run, :]
-        for k in range(1, slides):
-            slide_copy(k, zs.at[lax.rem(my_slide + k, slides)], zbuf.at[my_slide]).start()
-        zbuf[my_slide] = zs[my_slide]
         for k in range(1, slides):
             owner = lax.rem(my_slide + slides - k, slides)
             slide_copy(k, zbuf.at[owner], zbuf.at[owner]).wait_recv()
-        share = jnp.sum(zbuf[...], axis=0)[0:run, :]
+        summed = jnp.sum(zbuf[...].astype(F32), axis=0)
+        for k in range(chips):
+            cs[k, 0:run, :] = summed[k * run:(k + 1) * run, :]
+        for k in range(1, chips):
+            hop(7, k, across_chips(k), cs.at[lax.rem(chip + k, chips)], cbuf.at[chip]).start()
+        cbuf[chip] = cs[chip]
+        for k in range(1, chips):
+            block = cbuf.at[lax.rem(chip + chips - k, chips)]
+            hop(7, k, partner, block, block).wait_recv()
+        share = jnp.sum(cbuf[...], axis=0)[0:run, :]
         for j in range(d // 128):
             wgrad_ref[pl.ds(j, run, stride=d // 128), :] = share[:, j * 128:(j + 1) * 128]
         for k in range(1, slides):
             slide_copy(k, zs.at[0], zbuf.at[0]).wait_send()
-        left(7, lambda i: wbuf.at[i])
+        pair_copy.wait_send()
+        for k in range(1, chips):
+            hop(7, k, partner, cs.at[0], cs.at[0]).wait_send()
     left(0, lambda i: pbuf.at[i])
     for c in range(chunks):
         left(1 + c, lambda i, c=c: got.at[c, i])
@@ -419,16 +475,29 @@
         left(8 + c, lambda i, c=c: bsend.at[c, i])
 
 
-def finish(placing_ref, back_ref, far_in, *rest):
-    wgrad_in = rest[:(len(rest) - 2) // 2]
-    grads_ref, far_ref = rest[len(wgrad_in):len(wgrad_in) + 2]
-    grads_ref[...] = dot(placing_ref[...], back_ref[...]).astype(BF)
-
-    @pl.when(pl.program_id(0) == 0)
-    def small():
-        far_ref[...] = far_in[...] * math.sqrt(far_in.shape[2] * lax.axis_size("ctx"))
-        for source, target in zip(wgrad_in, rest[len(wgrad_in) + 2:]):
-            target[...] = source[...]
+def finish(placing_hbm, back_hbm, *refs):
+    count = (len(refs) - 6) // 2
+    small_in, (grads_hbm, *small_out) = refs[:count], refs[count:2 * count + 1]
+    placing_ref, back_ref, grads_ref, in_sems, out_sems, small_sems = refs[2 * count + 1:]
+    chunks = back_ref.shape[0]
+    wide = back_ref.shape[2]
+    loads = [pltpu.make_async_copy(placing_hbm, placing_ref, in_sems.at[chunks])]
+    stores = []
+    for c in range(chunks):
+        cols = slice(c * wide, (c + 1) * wide)
+        loads.append(pltpu.make_async_copy(back_hbm.at[:, cols], back_ref.at[c], in_sems.at[c]))
+        stores.append(pltpu.make_async_copy(grads_ref.at[c], grads_hbm.at[:, cols], out_sems.at[c]))
+    passed = [pltpu.make_async_copy(a, b, small_sems.at[i])
+              for i, (a, b) in enumerate(zip(small_in, small_out))]
+    for copy in loads + passed:
+        copy.start()
+    loads[0].wait()
+    for c in range(chunks):
+        loads[1 + c].wait()
+        grads_ref[c] = dot(placing_ref[...], back_ref[c]).astype(BF)
+        stores[c].start()
+    for copy in stores + passed:
+        copy.wait()
 
 
 def local(slides, n, tiles, tile_pos, lengths, qkv_weight, out_weight, cotangent):
@@ -437,10 +506,10 @@
     heads = hc // HD
     portion = t // n
     g = t // STRIDE
-    fused = hc % (n * slides) == 0 and (hc // n) % 16 == 0
+    fused = hc % (n * slides) == 0 and (hc // (2 * slides)) % 16 == 0
     run = hc // (n * slides) if fused else 0
     pad = -(-run // 8) * 8 if fused else 8
-    wrows = hc // n if fused else 16
+    wrows = hc // 2 if fused else 16
     chunks = 3
     wide = d // chunks
     fq = heads * g
@@ -457,8 +526,10 @@
         vm((n, g, 2 * hc), BF), vm((n, g, 2 * hc), BF), vm((128, t), F32), vm((n, g, 128), F32),
         vm((hc, t), F32), vm((heads // 2, t, 128), F32), vm((heads // 2, t, 128), F32),
         vm((chunks, n, portion, wide), BF),
-        vm((n, wrows, d), BF), vm((n, wrows, d), BF),
-        vm((slides, pad, d), F32), vm((slides, pad, d), F32),
+        vm((2, wrows, d), F32), vm((wrows, d), F32),
+        vm((slides, wrows // slides if fused else 16, d), BF),
+        vm((slides, wrows // slides if fused else 16, d), BF),
+        vm((n // 2, pad, d), F32), vm((n // 2, pad, d), F32),
         vm((fq, hc), BF), vm((fq, t), BF), vm((hc, hc), BF),
         dma((4,)), dma((1 + chunks,)), dma((8 + chunks, n)), dma((8 + chunks, n)),
         dma((slides,)), dma((slides,)),
@@ -481,24 +552,20 @@
         ),
         cost_estimate=pl.CostEstimate(flops=8 * 10**9, bytes_accessed=6 * 10**6, transcendentals=2 * 10**6),
     )(lengths, tile_pos, tiles[0], qkv_weight, out_weight, cotangent[0])
+    small = (far, wgrad) if fused else (far,)
     grads, far, *rest = pl.pallas_call(
         finish,
-        grid=(chunks,),
-        out_shape=(
-            jax.ShapeDtypeStruct((t, d), BF),
-            jax.ShapeDtypeStruct(far.shape, F32),
-        ) + ((jax.ShapeDtypeStruct(wgrad.shape, F32),) if fused else ()),
-        in_specs=[
-            pl.BlockSpec((t, t), lambda i: (0, 0)),
-            pl.BlockSpec((t, wide), lambda i: (0, i)),
-            pl.BlockSpec(far.shape, lambda i: (0, 0, 0, 0)),
-        ] + [pl.BlockSpec(wgrad.shape, lambda i: (0, 0))] * fused,
-        out_specs=(
-            pl.BlockSpec((t, wide), lambda i: (0, i)),
-            pl.BlockSpec(far.shape, lambda i: (0, 0, 0, 0)),
-        ) + (pl.BlockSpec(wgrad.shape, lambda i: (0, 0)),) * fused,
+        out_shape=(jax.ShapeDtypeStruct((t, d), BF),)
+        + tuple(jax.ShapeDtypeStruct(x.shape, F32) for x in small),
+        in_specs=[any_spec] * (2 + len(small)),
+        out_specs=(any_spec,) * (1 + len(small)),
+        scratch_shapes=[
+            vm((t, t), BF), vm((chunks, t, wide), BF), vm((chunks, t, wide), BF),
+            dma((chunks + 1,)), dma((chunks,)), dma((2,)),
+        ],
+        compiler_params=pltpu.CompilerParams(vmem_limit_bytes=56 * 1024 * 1024),
         cost_estimate=pl.CostEstimate(flops=2 * t * t * d, bytes_accessed=3 * 10**6, transcendentals=0),
-    )(placing, back.reshape(t, d), far, *([wgrad] * fused))
+    )(placing, back.reshape(t, d), *small)
     if fused:
         wgrad = rest[0].reshape(-1)
     else:

time: 51.3 us -> 57.4 us (1.12)
  Pallas kernels: 49.5 us -> 55.4 us
    pallas_call x1, Pallas kernels: 3.63 us -> 8.26 us  [local(): pl.pallas_call(finish, out_shape=(jax.ShapeDtypeStruct((t, d), BF),) + tu...]
    pallas_call x1, Pallas kernels: 45.9 us -> 47.1 us  [local(): pl.pallas_call(functools.partial(layer, n, slides, fused), out_shape=(jax...]
where the time goes in v4:
time: 57.4 us; the launch traced here: 56.8 us
  Pallas kernels  55.4 us (97%)
  between operations  1.45 us (3%)
    pallas_call x1, Pallas kernels, local(): pl.pallas_call(functools.partial(layer, n, slides, fused), out_shape=(jax...  47.1 us
    pallas_call x1, Pallas kernels, local(): pl.pallas_call(finish, out_shape=(jax.ShapeDtypeStruct((t, d), BF),) + tu...  8.26 us

profile of v4, /device:TPU:1, one launch (start us, length us, event | category | flops | bytes accessed | tf_op | source)
XLA Modules:
  0.0 56.8 jit_solution(8637906712665727770)
XLA Ops:
  1.3 47.1 %shard_map.85 = (bf16[8,64,768]{2,1,0:T(8,128)(2,1)}, bf16[512,512]{1,0:T(8,128)(2,1)}, f32[72,128]{1,0:T(8,128)}, f32[2,6,32,64]{3,2,1,0:T(8,128)}) custom-call(s32[1]{0:T(128)S(6)} %copy.9.len_ref, s32[1,512]{1,0:T(1,128)} %pos_ref.1, bf16[512,768]{1,0:T(8,128)(2,1)} %bitcast.7, bf16[768,1152]{1,0:T(8,128)(2,1)} %wqkv_hbm.1, bf16[384,768]{1,0:T(8,128)(2,1)} %wout_hbm.1, ...), custom_call_target="tpu_custom_call" | custom-call | flops 8000000000 | bytes 6000000 | tf_op jit(solution)/shard_map/pallas_call | solution.py:539
  48.4 8.3 %shard_map.86 = (bf16[512,768]{1,0:T(8,128)(2,1)}, f32[2,6,32,64]{3,2,1,0:T(8,128)}, f32[72,128]{1,0:T(8,128)}) custom-call(bf16[512,512]{1,0:T(8,128)(2,1)} %get-tuple-element.10.placing_hbm, bf16[512,768]{1,0:T(8,128)(2,1)} %bitcast.6, f32[2,6,32,64]{3,2,1,0:T(8,128)} %get-tuple-element.12.refs_0_, f32[72,128]{1,0:T(8,128)} %get-tuple-element.13.refs_1_), custom_call_target="tpu_custom_call" | custom-call | flops 402653184 | bytes 3000000 | tf_op jit(solution)/shard_map/pallas_call | solution.py:556

commit v5 on v3

--- a/solution.py
+++ b/solution.py
@@ -62,7 +62,7 @@
           sent, psend, got, pbuf, slot_ref, st_ref, rt_ref, acc, proj, g_ref, gt_ref, kt_ref,
           vt_ref, w_ref, dp_ref, m_ref, l_ref, nt_ref, att_ref, stat_ref, kvbuf, qgbuf, stats, sbuf,
           dqt_ref, dk_ref, dv_ref, bsend, pw, wbuf, zs, zbuf,
-          block_ref, spread_ref, order_ref,
+          block_ref, spread_ref, order_ref, bias_ref, wb_ref, ds_ref,
           in_sems, own_sems, send_sems, recv_sems, zsend, zrecv):
     me = lax.axis_index("ctx")
     my_slide = lax.axis_index("slide")
@@ -161,6 +161,7 @@
     lane = iota((1, 2 * HD), 1)
 
     pairs = heads // 2
+    bias_ref[...] = jnp.where(base + iota((t, 128), 0) < length, 0.0, FLOOR)
 
     def fill(ref, start, value):
         for pair in range(pairs):
@@ -233,23 +234,42 @@
     kt_ref[...] = flip(proj[:, hc:2 * hc])
     vt_ref[...] = flip(proj[:, 2 * hc:3 * hc])
 
-    for pair in range(heads // 2):
-        cols = slice(pair * 128, pair * 128 + 128)
-        q2 = proj[:, cols]
-        k2 = proj[:, hc + pair * 128:hc + pair * 128 + 128]
-        v2 = proj[:, 2 * hc + pair * 128:2 * hc + pair * 128 + 128]
-        for half in range(2):
-            h = 2 * pair + half
-            rows = slice(h * HD, h * HD + HD)
-            mine = hot(lane >> 6 == half)
-            score = jnp.where(live_col, dot_t(k2 * (mine * 0.125), q2), FLOOR)
-            top = jnp.maximum(jnp.max(score, axis=0, keepdims=True), 0.5 * FLOOR)
-            weight = jnp.exp(score - top)
-            w_ref[h] = weight
-            m_ref[h:h + 1, :] = top
-            l_ref[h:h + 1, :] = jnp.sum(weight, axis=0, keepdims=True)
-            nt_ref[rows, :] = dot(vt_ref[rows, :], weight.astype(BF))
-            dp_ref[h] = dot(v2 * mine, gt_ref[cols, :])
+    span = 64
+    pieces = [slice(r, r + span) for r in range(0, t, span)]
+
+    def dead(piece):
+        return jnp.concatenate([bias_ref[piece, :]] * (t // 128), axis=1)
+
+    def folded(x, combine):
+        return combine(x.reshape(span // 8, 8, t), axis=0)
+
+    def scores(h):
+        start = h // 2 * 128
+        mine = hot(lane >> 6 == h % 2)
+        w_ref[h] = dot_t(proj[:, hc + start:hc + start + 128] * (mine * 0.125),
+                         proj[:, start:start + 128])
+
+    scores(0)
+    for h in range(heads):
+        start = h // 2 * 128
+        rows = slice(h * HD, h * HD + HD)
+        if h + 1 < heads:
+            scores(h + 1)
+        dp_ref[h] = dot(proj[:, 2 * hc + start:2 * hc + start + 128] * hot(lane >> 6 == h % 2),
+                        gt_ref[start:start + 128, :])
+        top = jnp.full((8, t), 0.5 * FLOOR, F32)
+        for piece in pieces:
+            top = jnp.maximum(top, folded(w_ref[h, piece, :] + dead(piece), jnp.max))
+        top = jnp.max(top, axis=0, keepdims=True)
+        total = jnp.zeros((8, t), F32)
+        for piece in pieces:
+            weight = jnp.exp(w_ref[h, piece, :] + dead(piece) - top)
+            w_ref[h, piece, :] = weight
+            wb_ref[h % 2, piece, :] = weight.astype(BF)
+            total = total + folded(weight, jnp.sum)
+        m_ref[h:h + 1, :] = top
+        l_ref[h:h + 1, :] = jnp.sum(total, axis=0, keepdims=True)
+        nt_ref[rows, :] = dot(vt_ref[rows, :], wb_ref[h % 2])
 
     landed(4, lambda i: kvbuf.at[i])
     all_k = kvbuf[:, :, 0:hc].reshape(nf, hc)
@@ -331,11 +351,16 @@
         for half in range(2):
             h = 2 * pair + half
             rows = slice(h * HD, h * HD + HD)
-            prob = w_ref[h] * near_part[h:h + 1]
-            dscore = (prob * (dp_ref[h] - stat[h:h + 1])).astype(BF)
+            unit = near_part[h:h + 1]
+            own_stat = stat[h:h + 1]
+            for piece in pieces:
+                prob = w_ref[h, piece, :] * unit
+                wb_ref[half, piece, :] = prob.astype(BF)
+                ds_ref[half, piece, :] = (prob * (dp_ref[h, piece, :] - own_stat)).astype(BF)
+            dscore = ds_ref[half]
             dqt_ref[rows, :] = dot(kt_ref[rows, :] * 0.125, dscore)
             key_parts.append(dot(dscore, q2))
-            value_parts.append(dot(prob.astype(BF), g2))
+            value_parts.append(dot(wb_ref[half], g2))
         dk_ref[pair] = jnp.where(lane < HD, key_parts[0], key_parts[1])
         dv_ref[pair] = jnp.where(lane < HD, value_parts[0], value_parts[1])
 
@@ -380,7 +405,7 @@
 
     for which in range(2):
         for h in range(heads):
-            far_ref[which, h] = terms[which][h * g:(h + 1) * g, h * HD:(h + 1) * HD]
+            far_ref[which, h] = terms[which][h * g:(h + 1) * g, h * HD:(h + 1) * HD] * math.sqrt(nf)
 
     if fused:
         def slide_copy(k, src, dst):
@@ -419,16 +444,36 @@
         left(8 + c, lambda i, c=c: bsend.at[c, i])
 
 
-def finish(placing_ref, back_ref, far_in, *rest):
-    wgrad_in = rest[:(len(rest) - 2) // 2]
-    grads_ref, far_ref = rest[len(wgrad_in):len(wgrad_in) + 2]
-    grads_ref[...] = dot(placing_ref[...], back_ref[...]).astype(BF)
-
-    @pl.when(pl.program_id(0) == 0)
-    def small():
-        far_ref[...] = far_in[...] * math.sqrt(far_in.shape[2] * lax.axis_size("ctx"))
-        for source, target in zip(wgrad_in, rest[len(wgrad_in) + 2:]):
-            target[...] = source[...]
+def finish(placing_hbm, back_hbm, *refs):
+    count = (len(refs) - 7) // 3
+    small_in, (grads_hbm, *small_out) = refs[:count], refs[count:2 * count + 1]
+    placing_ref, back_ref, grads_ref, in_sems, out_sems, small_sems = refs[2 * count + 1:2 * count + 7]
+    held = refs[2 * count + 7:]
+    chunks = back_ref.shape[0]
+    wide = back_ref.shape[2]
+    loads = [pltpu.make_async_copy(placing_hbm, placing_ref, in_sems.at[chunks])]
+    stores = []
+    for c in range(chunks):
+        cols = slice(c * wide, (c + 1) * wide)
+        loads.append(pltpu.make_async_copy(back_hbm.at[:, cols], back_ref.at[c], in_sems.at[c]))
+        stores.append(pltpu.make_async_copy(grads_ref.at[c], grads_hbm.at[:, cols], out_sems.at[c]))
+    taken = [pltpu.make_async_copy(a, b, small_sems.at[0, i])
+             for i, (a, b) in enumerate(zip(small_in, held))]
+    given = [pltpu.make_async_copy(a, b, small_sems.at[1, i])
+             for i, (a, b) in enumerate(zip(held, small_out))]
+    for copy in loads + taken:
+        copy.start()
+    loads[0].wait()
+    for c in range(chunks):
+        loads[1 + c].wait()
+        grads_ref[c] = dot(placing_ref[...], back_ref[c]).astype(BF)
+        stores[c].start()
+        if c == 0:
+            for before, after in zip(taken, given):
+                before.wait()
+                after.start()
+    for copy in stores + given:
+        copy.wait()
 
 
 def local(slides, n, tiles, tile_pos, lengths, qkv_weight, out_weight, cotangent):
@@ -460,6 +505,7 @@
         vm((n, wrows, d), BF), vm((n, wrows, d), BF),
         vm((slides, pad, d), F32), vm((slides, pad, d), F32),
         vm((fq, hc), BF), vm((fq, t), BF), vm((hc, hc), BF),
+        vm((t, 128), F32), vm((2, t, t), BF), vm((2, t, t), BF),
         dma((4,)), dma((1 + chunks,)), dma((8 + chunks, n)), dma((8 + chunks, n)),
         dma((slides,)), dma((slides,)),
     ]
@@ -481,24 +527,20 @@
         ),
         cost_estimate=pl.CostEstimate(flops=8 * 10**9, bytes_accessed=6 * 10**6, transcendentals=2 * 10**6),
     )(lengths, tile_pos, tiles[0], qkv_weight, out_weight, cotangent[0])
+    small = (far, wgrad) if fused else (far,)
     grads, far, *rest = pl.pallas_call(
         finish,
-        grid=(chunks,),
-        out_shape=(
-            jax.ShapeDtypeStruct((t, d), BF),
-            jax.ShapeDtypeStruct(far.shape, F32),
-        ) + ((jax.ShapeDtypeStruct(wgrad.shape, F32),) if fused else ()),
-        in_specs=[
-            pl.BlockSpec((t, t), lambda i: (0, 0)),
-            pl.BlockSpec((t, wide), lambda i: (0, i)),
-            pl.BlockSpec(far.shape, lambda i: (0, 0, 0, 0)),
-        ] + [pl.BlockSpec(wgrad.shape, lambda i: (0, 0))] * fused,
-        out_specs=(
-            pl.BlockSpec((t, wide), lambda i: (0, i)),
-            pl.BlockSpec(far.shape, lambda i: (0, 0, 0, 0)),
-        ) + (pl.BlockSpec(wgrad.shape, lambda i: (0, 0)),) * fused,
+        out_shape=(jax.ShapeDtypeStruct((t, d), BF),)
+        + tuple(jax.ShapeDtypeStruct(x.shape, F32) for x in small),
+        in_specs=[any_spec] * (2 + len(small)),
+        out_specs=(any_spec,) * (1 + len(small)),
+        scratch_shapes=[
+            vm((t, t), BF), vm((chunks, t, wide), BF), vm((chunks, t, wide), BF),
+            dma((chunks + 1,)), dma((chunks,)), dma((2, 2)),
+        ] + [vm(x.shape, F32) for x in small],
+        compiler_params=pltpu.CompilerParams(vmem_limit_bytes=56 * 1024 * 1024),
         cost_estimate=pl.CostEstimate(flops=2 * t * t * d, bytes_accessed=3 * 10**6, transcendentals=0),
-    )(placing, back.reshape(t, d), far, *([wgrad] * fused))
+    )(placing, back.reshape(t, d), *small)
     if fused:
         wgrad = rest[0].reshape(-1)
     else:

time: 51.3 us -> 50.9 us (level)
    pallas_call x1, Pallas kernels: 3.63 us -> 3.06 us  [local(): pl.pallas_call(finish, out_shape=(jax.ShapeDtypeStruct((t, d), BF),) + tu...]
where the time goes in v5:
time: 50.9 us; the launch traced here: 50.4 us
  Pallas kernels  49 us (96%)
  between operations  1.45 us (3%)
    pallas_call x1, Pallas kernels, local(): pl.pallas_call(functools.partial(layer, n, slides, fused), out_shape=(jax...  45.9 us
    pallas_call x1, Pallas kernels, local(): pl.pallas_call(finish, out_shape=(jax.ShapeDtypeStruct((t, d), BF),) + tu...  3.06 us

profile of v5, /device:TPU:1, one launch (start us, length us, event | category | flops | bytes accessed | tf_op | source)
XLA Modules:
  0.0 50.4 jit_solution(14961270154311943709)
XLA Ops:
  1.3 45.9 %shard_map.85 = (bf16[8,64,768]{2,1,0:T(8,128)(2,1)}, bf16[512,512]{1,0:T(8,128)(2,1)}, f32[72,128]{1,0:T(8,128)}, f32[2,6,32,64]{3,2,1,0:T(8,128)}) custom-call(s32[1]{0:T(128)S(6)} %copy.9.len_ref, s32[1,512]{1,0:T(1,128)} %pos_ref.1, bf16[512,768]{1,0:T(8,128)(2,1)} %bitcast.7, bf16[768,1152]{1,0:T(8,128)(2,1)} %wqkv_hbm.1, bf16[384,768]{1,0:T(8,128)(2,1)} %wout_hbm.1, ...), custom_call_target="tpu_custom_call" | custom-call | flops 8000000000 | bytes 6000000 | tf_op jit(solution)/shard_map/pallas_call | solution.py:514
  47.2 3.1 %shard_map.86 = (bf16[512,768]{1,0:T(8,128)(2,1)}, f32[2,6,32,64]{3,2,1,0:T(8,128)}, f32[72,128]{1,0:T(8,128)}) custom-call(bf16[512,512]{1,0:T(8,128)(2,1)} %get-tuple-element.10.placing_hbm, bf16[512,768]{1,0:T(8,128)(2,1)} %bitcast.6, f32[2,6,32,64]{3,2,1,0:T(8,128)} %get-tuple-element.12.refs_0_, f32[72,128]{1,0:T(8,128)} %get-tuple-element.13.refs_1_), custom_call_target="tpu_custom_call" | custom-call | flops 402653184 | bytes 3000000 | tf_op jit(solution)/shard_map/pallas_call | solution.py:531

commit v6 on v5

--- a/solution.py
+++ b/solution.py
@@ -226,7 +226,6 @@
             picked = far_rows(k * pairs)
             if k == 0:
                 qgbuf[me, :, 0:hc] = picked
-                push(5, lambda peer: qgbuf.at[me], lambda i: qgbuf.at[i])
             else:
                 kvbuf[me, :, (k - 1) * hc:k * hc] = picked
             if k == 2:
@@ -272,6 +271,7 @@
         nt_ref[rows, :] = dot(vt_ref[rows, :], wb_ref[h % 2])
 
     landed(4, lambda i: kvbuf.at[i])
+    push(5, lambda peer: qgbuf.at[me], lambda i: qgbuf.at[i])
     all_k = kvbuf[:, :, 0:hc].reshape(nf, hc)
     all_v = kvbuf[:, :, hc:2 * hc].reshape(nf, hc)
     block = block_ref[...]

time: 50.9 us -> 52.9 us (1.039)
  Pallas kernels: 49 us -> 51.1 us
    pallas_call x1, Pallas kernels: 45.9 us -> 48 us  [local(): pl.pallas_call(functools.partial(layer, n, slides, fused), out_shape=(jax...]
where the time goes in v6:
time: 52.9 us; the launch traced here: 52.5 us
  Pallas kernels  51.1 us (97%)
  between operations  1.45 us (3%)
    pallas_call x1, Pallas kernels, local(): pl.pallas_call(functools.partial(layer, n, slides, fused), out_shape=(jax...  48 us
    pallas_call x1, Pallas kernels, local(): pl.pallas_call(finish, out_shape=(jax.ShapeDtypeStruct((t, d), BF),) + tu...  3.06 us

profile of v6, /device:TPU:1, one launch (start us, length us, event | category | flops | bytes accessed | tf_op | source)
XLA Modules:
  0.0 52.5 jit_solution(15457416212901873197)
XLA Ops:
  1.3 48.0 %shard_map.85 = (bf16[8,64,768]{2,1,0:T(8,128)(2,1)}, bf16[512,512]{1,0:T(8,128)(2,1)}, f32[72,128]{1,0:T(8,128)}, f32[2,6,32,64]{3,2,1,0:T(8,128)}) custom-call(s32[1]{0:T(128)S(6)} %copy.9.len_ref, s32[1,512]{1,0:T(1,128)} %pos_ref.1, bf16[512,768]{1,0:T(8,128)(2,1)} %bitcast.7, bf16[768,1152]{1,0:T(8,128)(2,1)} %wqkv_hbm.1, bf16[384,768]{1,0:T(8,128)(2,1)} %wout_hbm.1, ...), custom_call_target="tpu_custom_call" | custom-call | flops 8000000000 | bytes 6000000 | tf_op jit(solution)/shard_map/pallas_call | solution.py:514
  49.3 3.1 %shard_map.86 = (bf16[512,768]{1,0:T(8,128)(2,1)}, f32[2,6,32,64]{3,2,1,0:T(8,128)}, f32[72,128]{1,0:T(8,128)}) custom-call(bf16[512,512]{1,0:T(8,128)(2,1)} %get-tuple-element.10.placing_hbm, bf16[512,768]{1,0:T(8,128)(2,1)} %bitcast.6, f32[2,6,32,64]{3,2,1,0:T(8,128)} %get-tuple-element.12.refs_0_, f32[72,128]{1,0:T(8,128)} %get-tuple-element.13.refs_1_), custom_call_target="tpu_custom_call" | custom-call | flops 402653184 | bytes 3000000 | tf_op jit(solution)/shard_map/pallas_call | solution.py:531
